TPU v7x, 512 devices: a whole 4x8x8 slice. The times are simulated.
512 devices in a mesh: dp: 32 (over z, y_hi), segment: 2 (over y_lo), mp: 8 (over x, core).
Axes of the slice: x: 4, y: 8 (y_hi: 4, y_lo: 2; y = y_hi * 2 + y_lo), z: 8, core: 2. Of those that a mesh axis runs over, the one named last changes fastest.
Arguments:
- prefix_hidden: bfloat16 [64, 512, 8192], P(('dp', 'segment'), 'mp'), may hold values from -16 to 16
- norm_gain: float32 [8192], replicated, may hold values from 0.5 to 1.5
- kv_weight: bfloat16 [8192, 2, 1024], P('dp', None, 'mp'), may hold values from -0.0625 to 0.0625
- action_query: bfloat16 [64, 128, 2048], P(('dp', 'segment'), None, 'mp'), may hold values from -104 to 104
- action_kv: bfloat16 [64, 128, 2, 1024], P(('dp', 'segment'), None, None, 'mp'), may hold values from -4.25 to 4.25
- out_cotangent: bfloat16 [64, 128, 2048], P(('dp', 'segment'), None, 'mp'), may hold values from -18 to 18
- prefix_blocks: int32 [64, 512], P(('dp', 'segment')), may hold values from 0 to 7, as said below
- action_blocks: int32 [64, 128], P(('dp', 'segment')), may hold values from 0 to 8, as said below
- prefix_lengths: int32 [64], P(('dp', 'segment')), may hold values from 128 to 512, as said below
- timesteps: int32 [64], P(('dp', 'segment')), may hold values from 0 to 999
Outputs:
- attn_out: bfloat16 [64, 128, 2048], P(('dp', 'segment'), None, 'mp')
- query_grad: float32 [64, 128, 2048], P(('dp', 'segment'), None, 'mp')
- action_kv_grad: float32 [64, 128, 2, 1024], P(('dp', 'segment'), None, None, 'mp')
- weight_grad: float32 [8192, 2, 1024], P('dp', None, 'mp')
Inputs may be any that keep to these rules, and one draw needn't show every extreme that they name: `prefix_blocks`: constant over each run of 64 positions, 0 on the first run, rising by 0 or 1 from one run to the next; in every draw some sample rises at every run. `action_blocks`: constant over each run of 64 positions; the last run of every sample holds 8; in every draw some sample's first run holds 0. `prefix_lengths`: in every draw some sample's prefix is whole and some sample's is 128.
All inputs are finite; a program needn't handle non-finite values.
Results may differ from a plain program's by a relative error of at most 0.017.
Values may be sent and summed in bfloat16 or wider, within the bound.
No kernel may reach another device: no remote copies, remote signals or barrier semaphores. Data moves between devices by JAX's collectives and lax.ppermute only.
A program may use at most 64 MiB of HBM per device.

v0:
```python
import jax
import jax.numpy as jnp
from jax import lax
from jax.sharding import Mesh
from jax.sharding import PartitionSpec as P

KVH = 8
HD = 128
QH = 16
STEPS = 1000
DP = ("dp_0", "dp_1")
DP_SEGMENT = ("dp_0", "dp_1", "segment")


EPS = 1e-06
NEGATIVE = -1e30


def sum_by_axis(terms, axes):
    subtotal = terms.astype(jnp.bfloat16)
    for axis in axes:
        subtotal = lax.psum_scatter(subtotal, axis, scatter_dimension=0, tiled=True)
    return subtotal.astype(jnp.float32)


def from_everyone(array, axis):
    copies = jnp.broadcast_to(array, (lax.axis_size(axis), *array.shape))
    return lax.all_to_all(copies, axis, split_axis=0, concat_axis=0, tiled=True)


def taken_together(array, axis):
    everything = from_everyone(array, axis)
    return jnp.sum(everything.astype(jnp.float32), axis=0)


def head_scores(query, keys):
    return jnp.einsum("agrh,jgh->graj", query, keys, preferred_element_type=jnp.float32) * HD ** (
        -0.5
    )


def backward_terms(probs, values, keys, query, grad_out):
    probs_low = probs.astype(jnp.bfloat16)
    d_probs = jnp.einsum("agrh,jgh->graj", grad_out, values, preferred_element_type=jnp.float32)
    delta = jnp.sum(probs * d_probs, axis=-1, keepdims=True)
    d_scores = (probs * (d_probs - delta)).astype(jnp.bfloat16)
    d_query = jnp.einsum(
        "graj,jgh->agrh", d_scores, keys, preferred_element_type=jnp.float32
    ) * HD ** (-0.5)
    d_keys = jnp.einsum(
        "graj,agrh->jgh", d_scores, query, preferred_element_type=jnp.float32
    ) * HD ** (-0.5)
    d_values = jnp.einsum("graj,agrh->jgh", probs_low, grad_out, preferred_element_type=jnp.float32)
    return (d_query, jnp.stack([d_keys, d_values], axis=1))


def shards(
    prefix_hidden,
    norm_gain,
    kv_weight,
    action_query,
    action_kv,
    out_cotangent,
    prefix_blocks,
    action_blocks,
    prefix_lengths,
    timesteps,
):
    acts = action_query.shape[1]
    heads_kv = kv_weight.shape[2] // HD
    ratio = QH // KVH
    columns = 2 * kv_weight.shape[2]
    wide = prefix_hidden[0].astype(jnp.float32)
    inverse = lax.rsqrt(jnp.mean(wide * wide, axis=-1, keepdims=True) + EPS)
    normed_local = (wide * inverse * norm_gain).astype(jnp.bfloat16)
    normed = lax.all_gather(normed_local, "mp", axis=0, tiled=True)
    rows = normed.shape[0]
    piece = lax.all_gather(kv_weight, DP, axis=0, tiled=True)
    section = normed
    projected = jnp.dot(
        section, piece.reshape(piece.shape[0], columns), preferred_element_type=jnp.float32
    )
    prefix_kv = projected.astype(jnp.bfloat16).reshape(rows, 2, heads_kv, HD)
    own_pair = action_kv[0].reshape(acts, 2, heads_kv, HD)
    query = action_query[0].reshape(acts, heads_kv, ratio, HD)
    flow_weight = 0.5 + (timesteps[0].astype(jnp.float32) + 0.5) / STEPS
    grad_out = (
        (flow_weight * out_cotangent[0].astype(jnp.float32))
        .astype(jnp.bfloat16)
        .reshape(acts, heads_kv, ratio, HD)
    )
    pblocks = prefix_blocks[0]
    ablocks = action_blocks[0]
    length = prefix_lengths[0]
    keys = jnp.concatenate([prefix_kv[:, 0], own_pair[:, 0]], axis=0)
    values = jnp.concatenate([prefix_kv[:, 1], own_pair[:, 1]], axis=0)
    positions = jnp.arange(rows, dtype=jnp.int32)
    see_prefix = (pblocks[None, :] <= ablocks[:, None]) & (positions[None, :] < length)
    see_action = ablocks[None, :] <= ablocks[:, None]
    visible = jnp.concatenate([see_prefix, see_action], axis=1)
    masked = jnp.where(visible, head_scores(query, keys), NEGATIVE)
    top = jnp.max(masked, axis=-1, keepdims=True)
    expo = jnp.where(visible, jnp.exp(masked - top), 0.0)
    probs = expo / jnp.sum(expo, axis=-1, keepdims=True)
    out = jnp.einsum(
        "graj,jgh->agrh", probs.astype(jnp.bfloat16), values, preferred_element_type=jnp.float32
    )
    d_query, d_pair = backward_terms(probs, values, keys, query, grad_out)
    d_prefix = d_pair[:rows]
    d_action = d_pair[rows:]
    attn_out = out.astype(jnp.bfloat16).reshape(1, acts, ratio * heads_kv * HD)
    query_grad = d_query.reshape(1, acts, ratio * heads_kv * HD)
    action_kv_grad = d_action.reshape(1, acts, 2, heads_kv * HD)
    prefix_grad = d_prefix.astype(jnp.bfloat16).reshape(rows, columns)
    section = normed
    term = lax.dot_general(
        section, prefix_grad, (((0,), (0,)), ((), ())), preferred_element_type=jnp.float32
    )
    shard = sum_by_axis(term.reshape(kv_weight.shape[0] * lax.axis_size(DP), 2, columns // 2), DP)
    weight_grad = taken_together(shard.astype(jnp.bfloat16), "segment").astype(jnp.float32)
    return (attn_out, query_grad, action_kv_grad, weight_grad)


def solution(mesh):
    torus = Mesh(
        mesh.devices.reshape(8, 4, mesh.shape["segment"], mesh.shape["mp"]),
        ("dp_0", "dp_1", "segment", "mp"),
    )
    placed = (
        P(DP_SEGMENT, "mp", None),
        P(),
        P(DP, None, "mp"),
        P(DP_SEGMENT, None, "mp"),
        P(DP_SEGMENT, None, None, "mp"),
        P(DP_SEGMENT, None, "mp"),
        P(DP_SEGMENT, None),
        P(DP_SEGMENT, None),
        P(DP_SEGMENT),
        P(DP_SEGMENT),
    )
    return jax.shard_map(
        shards,
        mesh=torus,
        in_specs=placed,
        out_specs=(
            P(DP_SEGMENT, None, "mp"),
            P(DP_SEGMENT, None, "mp"),
            P(DP_SEGMENT, None, None, "mp"),
            P(DP, None, "mp"),
        ),
        check_vma=False,
    )
```

profile of v0, /device:TPU:18, one launch (start us, length us, event | category | flops | bytes accessed | tf_op | source)
XLA Modules:
  0.0 294.3 jit_solution(14425961718619464857)
XLA Ops:
  7.3 0.7 all-gather.5.cloned.1.call-update
  8.0 1.5 fusion.4
  9.5 2.6 fusion.6
  14.3 102.6 %all-gather.5.cloned.1.call-done = bf16[8192,2,128]{2,1,0:T(2,128)(2,1)} async-done(((bf16[256,2,128]{2,1,0:T(2,128)(2,1)}), bf16[8192,2,128]{2,1,0:T(2,128)(2,1)}) %all-gather.5.cloned.1.call-update) | async-done | bytes 4194320 | tf_op jit(solution)/shard_map/all_gather | solution.py:78
  116.9 54.1 %all-gather.3.cloned.1.call-done = bf16[512,8192]{1,0:T(8,128)(2,1)} async-done(((bf16[64,8192]{1,0:T(8,128)(2,1)}), bf16[512,8192]{1,0:T(8,128)(2,1)}) %all-gather.3.cloned.1.call-update) | async-done | bytes 8388624 | tf_op jit(solution)/shard_map/all_gather | solution.py:76
  170.9 6.9 %fusion.8 = bf16[512,256]{0,1:T(8,128)(2,1)S(1)} fusion(bf16[512,8192]{1,0:T(8,128)(2,1)} %all-gather.3.cloned.1.call-done, bf16[1024,8,2,128]{3,2,1,0:T(2,128)(2,1)} %bitcast.129), kind=kOutput, calls=%fused_computation.13 | convolution fusion | flops 2147614720 | bytes 12845056 | tf_op jit(solution)/shard_map/dot_general | solution.py:80
  178.0 0.3 fusion.33
  178.5 0.3 convolution_bitcast_fusion.1
  178.8 0.3 multiply_reduce_fusion
  179.1 0.2 fusion.17
  179.3 0.2 fusion.13
  179.6 2.3 copy-done.5
  181.8 4.0 %convolution_convert_fusion = bf16[8192,2,128]{2,0,1:T(8,128)(2,1)} fusion(bf16[512,8192]{1,0:T(8,128)(2,1)S(1)} %copy-done.5, f32[640,1,1,128]{0,3,2,1:T(8,128)S(1)} %convolution_bitcast_fusion.1, f32[640,1,1,128]{0,3,2,1:T(8,128)S(1)} %fusion.13), kind=kOutput, calls=%fused_computation | convolution fusion | flops 2150105088 | bytes 13238272 | tf_op jit(solution)/shard_map/dot_general | solution.py:116
  185.9 59.9 %reduce-scatter.3.cloned.1.call-done = bf16[1024,2,128]{2,0,1:T(8,128)(2,1)} async-done(((bf16[8192,2,128]{2,0,1:T(8,128)(2,1)}), bf16[1024,2,128]{2,0,1:T(8,128)(2,1)}) %reduce-scatter.3.cloned.1.call-update) | async-done | bytes 524304 | tf_op jit(solution)/shard_map/reduce_scatter | solution.py:22
  245.8 0.3 convolution_convert_fusion.1
  246.1 0.7 copy.64
  246.8 29.7 %reduce-scatter.5.cloned.1.call-done = bf16[256,2,128]{2,0,1:T(8,128)(2,1)} async-done(((bf16[1024,2,128]{2,0,1:T(8,128)(2,1)}), bf16[256,2,128]{2,0,1:T(8,128)(2,1)}) %reduce-scatter.5.cloned.1.call-update) | async-done | bytes 131088 | tf_op jit(solution)/shard_map/reduce_scatter | solution.py:22
  276.6 1.6 broadcast_in_dim.24
  278.2 3.4 %all-to-all-start = ((bf16[2,256,2,128]{3,1,2,0:T(8,128)(2,1)}), bf16[2,256,2,128]{3,1,2,0:T(8,128)(2,1)S(1)}, u32[]{:S(2)}, u32[]{:S(2)}) async-start(bf16[2,256,2,128]{3,1,2,0:T(8,128)(2,1)} %broadcast_in_dim.24), calls=%async_computation.2 | async-start | bytes 524288 | tf_op jit(solution)/shard_map/all_to_all | solution.py:28
  281.7 0.3 convolution_multiply_fusion.1
  281.9 0.8 copy.65
  282.7 0.8 copy.66
  283.4 3.4 %all-to-all-done = bf16[2,256,2,128]{3,1,2,0:T(8,128)(2,1)S(1)} async-done(((bf16[2,256,2,128]{3,1,2,0:T(8,128)(2,1)}), bf16[2,256,2,128]{3,1,2,0:T(8,128)(2,1)S(1)}, u32[]{:S(2)}, u32[]{:S(2)}) %all-to-all-start) | async-done | bytes 262176 | tf_op jit(solution)/shard_map/all_to_all | solution.py:28
  286.8 0.9 copy.67
  (35 shorter events, 1.2 us)
Async XLA Ops:
  7.2 5.0 %copy-start = (bf16[1,128,2,128]{3,2,1,0:T(2,128)(2,1)S(1)}, bf16[1,128,2,128]{3,2,1,0:T(2,128)(2,1)}, u32[]{:S(2)}) copy-start(bf16[1,128,2,128]{3,2,1,0:T(2,128)(2,1)} %param.14) | copy-start | bytes 196612
  7.2 5.2 %copy-start.1 = (bf16[1,128,256]{2,1,0:T(8,128)(2,1)S(1)}, bf16[1,128,256]{2,1,0:T(8,128)(2,1)}, u32[]{:S(2)}) copy-start(bf16[1,128,256]{2,1,0:T(8,128)(2,1)} %param.13) | copy-start | bytes 196612
  7.2 6.6 %copy-start.2 = (bf16[1,128,256]{2,1,0:T(8,128)(2,1)S(1)}, bf16[1,128,256]{2,1,0:T(8,128)(2,1)}, u32[]{:S(2)}) copy-start(bf16[1,128,256]{2,1,0:T(8,128)(2,1)} %param.15) | copy-start | bytes 196612
  7.2 6.8 %copy-start.3 = (s32[1,128]{1,0:T(1,128)S(1)}, s32[1,128]{1,0:T(1,128)}, u32[]{:S(2)}) copy-start(s32[1,128]{1,0:T(1,128)} %param.17) | copy-start | bytes 1540
  7.2 6.9 %copy-start.4 = (s32[1,512]{1,0:T(1,128)S(1)}, s32[1,512]{1,0:T(1,128)}, u32[]{:S(2)}) copy-start(s32[1,512]{1,0:T(1,128)} %param.16) | copy-start | bytes 6148
  7.2 109.6 %all-gather.5.cloned.1.call-start = ((), (), s32[]{:S(2)}) async-start(), calls=%async_computation.4 | async-start | bytes 4325376 | tf_op jit(solution)/shard_map/all_gather | solution.py:78
  8.0 163.0 %all-gather.3.cloned.1.call-start = ((), (), s32[]{:S(2)}) async-start(), calls=%async_computation.3 | async-start | bytes 9437184 | tf_op jit(solution)/shard_map/all_gather | solution.py:76
  12.2 233.6 %reduce-scatter.3.cloned.1.call-start = ((), (), s32[]{:S(2)}) async-start(), calls=%async_computation.5 | async-start | bytes 4718592 | tf_op jit(solution)/shard_map/reduce_scatter | solution.py:22
  178.5 3.4 %copy-start.5 = (bf16[512,8192]{1,0:T(8,128)(2,1)S(1)}, bf16[512,8192]{1,0:T(8,128)(2,1)}, u32[]{:S(2)}) copy-start(bf16[512,8192]{1,0:T(8,128)(2,1)} %all-gather.3.cloned.1.call-done) | copy-start | bytes 25165828
  185.8 90.7 %reduce-scatter.5.cloned.1.call-start = ((), (), s32[]{:S(2)}) async-start(), calls=%async_computation.6 | async-start | bytes 655360 | tf_op jit(solution)/shard_map/reduce_scatter | solution.py:22
  278.2 8.6 %all-to-all-start = ((bf16[2,256,2,128]{3,1,2,0:T(8,128)(2,1)}), bf16[2,256,2,128]{3,1,2,0:T(8,128)(2,1)S(1)}, u32[]{:S(2)}, u32[]{:S(2)}) async-start(bf16[2,256,2,128]{3,1,2,0:T(8,128)(2,1)} %broadcast_in_dim.24), calls=%async_computation.2 | async-start | bytes 524288 | tf_op jit(solution)/shard_map/all_to_all | solution.py:28
Sparse Core Ops, SparseCore 0:
  11.2 105.6 all-gather.4
  119.0 51.8 all-gather.2
  185.9 59.7 reduce-scatter.2
  248.4 28.1 reduce-scatter.4
where the time goes:
time: 295 us; the launch traced here: 294 us
  waiting for transfers between devices  250 us (85%)
  between operations  15.3 us (5%)
  matrix products  12.6 us (4%)
  local copies, waits for them, and re-layouts  7.58 us (3%)
  other arithmetic  4.84 us (2%)
  starting transfers between devices  3.6 us (1%)
    all_gather x1, waiting for transfers between devices, shards(): piece = lax.all_gather(kv_weight, DP, axis=0, tiled=True)  103 us
    reduce_scatter x2, waiting for transfers between devices, sum_by_axis(): subtotal = lax.psum_scatter(subtotal, axis, scatter_dimension=0, tiled=True)  89.6 us
    all_gather x1, waiting for transfers between devices, shards(): normed = lax.all_gather(normed_local, 'mp', axis=0, tiled=True)  54.1 us
    dot_general x1, matrix products, shards(): jnp.dot(section, piece.reshape(piece.shape[0], columns), preferred_elemen...  6.94 us
  transfers between devices with their start and end apart: 5, of which 5 were waited for; matrix products, arithmetic and copies ran while one was open for 3% of the time, Pallas kernels for 0%

commit v1 on v0

--- a/solution.py
+++ b/solution.py
@@ -9,6 +9,8 @@
 QH = 16
 STEPS = 1000
 DP = ("dp_0", "dp_1")
+EVERY = ("dp_0", "dp_1", "segment", "mp")
+RING = 8
 DP_SEGMENT = ("dp_0", "dp_1", "segment")
 
 
@@ -16,21 +18,30 @@
 NEGATIVE = -1e30
 
 
-def sum_by_axis(terms, axes):
-    subtotal = terms.astype(jnp.bfloat16)
-    for axis in axes:
-        subtotal = lax.psum_scatter(subtotal, axis, scatter_dimension=0, tiled=True)
-    return subtotal.astype(jnp.float32)
+def rings(along_z_core):
+    groups = []
+    for x in range(4):
+        for core in range(2):
+            for other in range(RING):
+                places = [
+                    (k, other) if core == along_z_core else (other, k) for k in range(RING)
+                ]
+                groups.append([((z * RING + y) * 4 + x) * 2 + core for z, y in places])
+    return groups
 
 
-def from_everyone(array, axis):
-    copies = jnp.broadcast_to(array, (lax.axis_size(axis), *array.shape))
-    return lax.all_to_all(copies, axis, split_axis=0, concat_axis=0, tiled=True)
+FIRST = rings(0)
+SECOND = rings(1)
 
 
-def taken_together(array, axis):
-    everything = from_everyone(array, axis)
-    return jnp.sum(everything.astype(jnp.float32), axis=0)
+def exchange(parts, groups):
+    return lax.all_to_all(
+        parts, EVERY, split_axis=0, concat_axis=0, tiled=True, axis_index_groups=groups
+    )
+
+
+def from_ring(array, groups):
+    return exchange(jnp.broadcast_to(array, (RING, *array.shape)), groups)
 
 
 def head_scores(query, keys):
@@ -73,12 +84,19 @@
     wide = prefix_hidden[0].astype(jnp.float32)
     inverse = lax.rsqrt(jnp.mean(wide * wide, axis=-1, keepdims=True) + EPS)
     normed_local = (wide * inverse * norm_gain).astype(jnp.bfloat16)
+    side = lax.axis_index("segment")
+    core = lax.axis_index("mp") % 2
+    local = kv_weight.reshape(kv_weight.shape[0], columns)
+    normed_local, local = lax.optimization_barrier((normed_local, local))
     normed = lax.all_gather(normed_local, "mp", axis=0, tiled=True)
     rows = normed.shape[0]
-    piece = lax.all_gather(kv_weight, DP, axis=0, tiled=True)
+    part = local.shape[0] // 2
+    local = lax.dynamic_slice_in_dim(local, side * part, part, axis=0)
+    plane = from_ring(from_ring(local, FIRST), SECOND)
+    piece = jnp.where(core == 0, plane.swapaxes(0, 1), plane).reshape(RING * RING * part, columns)
     section = normed
     projected = jnp.dot(
-        section, piece.reshape(piece.shape[0], columns), preferred_element_type=jnp.float32
+        section, piece, preferred_element_type=jnp.float32
     )
     prefix_kv = projected.astype(jnp.bfloat16).reshape(rows, 2, heads_kv, HD)
     own_pair = action_kv[0].reshape(acts, 2, heads_kv, HD)
@@ -116,8 +134,18 @@
     term = lax.dot_general(
         section, prefix_grad, (((0,), (0,)), ((), ())), preferred_element_type=jnp.float32
     )
-    shard = sum_by_axis(term.reshape(kv_weight.shape[0] * lax.axis_size(DP), 2, columns // 2), DP)
-    weight_grad = taken_together(shard.astype(jnp.bfloat16), "segment").astype(jnp.float32)
+    term = term.astype(jnp.bfloat16).reshape(RING, RING, part, columns)
+    term = jnp.where(core == 0, term.swapaxes(0, 1), term).reshape(RING * RING * part, columns)
+    ring_sum = lax.psum_scatter(
+        term, EVERY, scatter_dimension=0, tiled=True, axis_index_groups=SECOND
+    )
+    terms = exchange(ring_sum.reshape(RING, part, columns), FIRST)
+    own = jnp.sum(terms.astype(jnp.float32), axis=0).astype(jnp.bfloat16)
+    theirs = lax.ppermute(own, "segment", [(0, 1), (1, 0)])
+    low = jnp.where(side == 0, own, theirs)
+    high = jnp.where(side == 0, theirs, own)
+    weight_grad = jnp.concatenate([low, high], axis=0).astype(jnp.float32)
+    weight_grad = weight_grad.reshape(kv_weight.shape)
     return (attn_out, query_grad, action_kv_grad, weight_grad)
 
 

time: 295 us -> 194 us (0.66)
  the two profiles are of different devices: /device:TPU:18 before, /device:TPU:2 now
where the time goes in v1:
time: 194 us; the launch traced here: 193 us
  waiting for transfers between devices  102 us (53%)
  blocking collectives  23.4 us (12%)
  starting transfers between devices  17.7 us (9%)
  between operations  15.6 us (8%)
  other arithmetic  15.3 us (8%)
  matrix products  11 us (6%)
  local copies, waits for them, and re-layouts  8.51 us (4%)
    all_to_all x2, waiting for transfers between devices, exchange(): lax.all_to_all(parts, EVERY, split_axis=0, concat_axis=0, tiled=True, axi...  63.4 us
    reduce_scatter x1, waiting for transfers between devices, shards(): lax.psum_scatter(term, EVERY, scatter_dimension=0, tiled=True, axis_index...  37.4 us
    all_to_all x1, blocking collectives, exchange(): lax.all_to_all(parts, EVERY, split_axis=0, concat_axis=0, tiled=True, axi...  23.4 us
    all_to_all x2, starting transfers between devices, exchange(): lax.all_to_all(parts, EVERY, split_axis=0, concat_axis=0, tiled=True, axi...  14.6 us
    select_n x1, other arithmetic, shards(): jnp.where(core == 0, plane.swapaxes(0, 1), plane)  7.28 us
    dot_general x1, matrix products, shards(): projected = jnp.dot(section, piece, preferred_element_type=jnp.float32)  6.94 us
    unnamed x18, local copies, waits for them, and re-layouts  5.58 us
  transfers between devices with their start and end apart: 5, of which 4 were waited for; matrix products, arithmetic and copies ran while one was open for 7% of the time, Pallas kernels for 0%

profile of v1, /device:TPU:2, one launch (start us, length us, event | category | flops | bytes accessed | tf_op | source)
XLA Modules:
  0.0 193.4 jit_solution(6146533236272717816)
XLA Ops:
  7.2 1.5 fusion
  8.8 0.9 copy.49
  9.7 2.5 %fusion.2 = bf16[64,8192]{1,0:T(8,128)(2,1)} fusion(bf16[1,64,8192]{2,1,0:T(8,128)(2,1)} %param.10, f32[8192]{0:T(1024)} %param.11, f32[64]{0:T(128)S(1)} %add_rsqrt_fusion), kind=kLoop, calls=%fused_computation.7 | loop fusion | flops 2097152 | bytes 2130176 | tf_op jit(solution)/shard_map/convert_element_type | solution.py:86
  12.3 23.4 %all_to_all.15 = bf16[8,128,256]{2,1,0:T(8,128)(2,1)S(1)} all-to-all(bf16[8,128,256]{2,1,0:T(8,128)(2,1)S(1)} %broadcast_in_dim.24), channel_id=1, replica_groups={{0,64,128,192,256,320,384,448},{8,72,136,200,264,328,392,456},{16,80,14..., dimensions={0} | all-to-all | bytes 1048576 | tf_op jit(solution)/shard_map/all_to_all | solution.py:38
  35.7 2.5 %broadcast_in_dim.25 = bf16[8,8,128,256]{3,2,1,0:T(8,128)(2,1)} broadcast(bf16[8,128,256]{2,1,0:T(8,128)(2,1)S(1)} %all_to_all.15), dimensions={1,2,3} | broadcast | bytes 4718592 | tf_op jit(solution)/shard_map/broadcast_in_dim | solution.py:44
  38.2 7.2 %all-to-all-start.1 = ((bf16[8,8,128,256]{3,2,1,0:T(8,128)(2,1)}), bf16[8,8,128,256]{3,2,1,0:T(8,128)(2,1)}, u32[]{:S(2)}, u32[]{:S(2)}) async-start(bf16[8,8,128,256]{3,2,1,0:T(8,128)(2,1)} %broadcast_in_dim.25), calls=%async_computation.1 | async-start | bytes 8388608 | tf_op jit(solution)/shard_map/all_to_all | solution.py:38
  47.6 50.7 %all-to-all-done.1 = bf16[8,8,128,256]{3,2,1,0:T(8,128)(2,1)} async-done(((bf16[8,8,128,256]{3,2,1,0:T(8,128)(2,1)}), bf16[8,8,128,256]{3,2,1,0:T(8,128)(2,1)}, u32[]{:S(2)}, u32[]{:S(2)}) %all-to-all-start.1) | async-done | bytes 4194336 | tf_op jit(solution)/shard_map/all_to_all | solution.py:38
  98.3 7.3 %copy_select_fusion = bf16[8,8,128,256]{3,2,1,0:T(8,128)(2,1)} fusion(bf16[8,8,128,256]{3,2,1,0:T(8,128)(2,1)} %all-to-all-done.1, pred[]{:T(512)S(6)} %eq.10), kind=kLoop, calls=%fused_computation.2 | loop fusion | flops 2097152 | bytes 8388609 | tf_op jit(solution)/shard_map/jit(_where)/select_n | solution.py:96
  105.6 6.9 %convolution_convert_fusion.1 = bf16[512,256]{0,1:T(8,128)(2,1)S(1)} fusion(bf16[512,8192]{1,0:T(8,128)(2,1)} %all-gather.2.cloned.1.call-done, bf16[8192,256]{1,0:T(8,128)(2,1)} %bitcast.117), kind=kOutput, calls=%fused_computation.11 | convolution fusion | flops 2147614720 | bytes 12845056 | tf_op jit(solution)/shard_map/dot_general | solution.py:98
  113.1 0.3 convolution_bitcast_fusion.1
  113.5 0.3 multiply_reduce_fusion
  114.3 2.2 %copy-done.5 = bf16[512,8192]{1,0:T(8,128)(2,1)S(1)} copy-done((bf16[512,8192]{1,0:T(8,128)(2,1)S(1)}, bf16[512,8192]{1,0:T(8,128)(2,1)}, u32[]{:S(2)}) %copy-start.5) | copy-done | bytes 8388632
  116.5 2.4 %convolution_convert_fusion = bf16[8192,256]{1,0:T(8,128)(2,1)S(1)} fusion(bf16[512,8192]{1,0:T(8,128)(2,1)S(1)} %copy-done.5, bf16[512,256]{0,1:T(8,128)(2,1)S(1)} %bitcast.124), kind=kOutput, calls=%fused_computation | convolution fusion | flops 2149580800 | bytes 12845056 | tf_op jit(solution)/shard_map/dot_general | solution.py:134
  118.9 2.4 %bitcast_select_fusion = bf16[8,8,128,256]{3,2,1,0:T(8,128)(2,1)} fusion(bf16[8,8,128,256]{3,2,1,0:T(8,128)(2,1)S(1)} %bitcast.118, pred[]{:T(512)S(6)} %eq.10), kind=kLoop, calls=%fused_computation.1 | loop fusion | flops 2097152 | bytes 8388609 | tf_op jit(solution)/shard_map/jit(_where)/select_n | solution.py:138
  121.3 37.4 %reduce-scatter.2.cloned.1.call-done = bf16[1024,256]{1,0:T(8,128)(2,1)} async-done(((bf16[8192,256]{1,0:T(8,128)(2,1)}), bf16[1024,256]{1,0:T(8,128)(2,1)}) %reduce-scatter.2.cloned.1.call-update) | async-done | bytes 524304 | tf_op jit(solution)/shard_map/reduce_scatter | solution.py:139
  158.7 7.4 %all-to-all-start.2 = ((bf16[8,128,256]{2,1,0:T(8,128)(2,1)}), bf16[8,128,256]{2,1,0:T(8,128)(2,1)S(1)}, u32[]{:S(2)}, u32[]{:S(2)}) async-start(bf16[8,128,256]{2,1,0:T(8,128)(2,1)} %bitcast.122), calls=%async_computation.3 | async-start | bytes 1048576 | tf_op jit(solution)/shard_map/all_to_all | solution.py:38
  166.4 0.3 convolution_convert_fusion.2
  166.7 12.7 %all-to-all-done.2 = bf16[8,128,256]{2,1,0:T(8,128)(2,1)S(1)} async-done(((bf16[8,128,256]{2,1,0:T(8,128)(2,1)}), bf16[8,128,256]{2,1,0:T(8,128)(2,1)S(1)}, u32[]{:S(2)}, u32[]{:S(2)}) %all-to-all-start.2) | async-done | bytes 524320 | tf_op jit(solution)/shard_map/all_to_all | solution.py:38
  179.5 3.0 %collective-permute-start = (bf16[128,256]{1,0:T(8,128)(2,1)S(1)}, bf16[128,256]{1,0:T(8,128)(2,1)S(1)}, u32[]{:S(2)}, u32[]{:S(2)}) collective-permute-start(bf16[128,256]{1,0:T(8,128)(2,1)S(1)} %reduce_sum.42), channel_id=1, source_target_pairs={{0,8},{8,0},{1,9},{9,1},{2,10},{10,2},{3,11},{11,3},{4,12},{12,4},... | collective-permute-start | bytes 196616 | tf_op jit(solution)/shard_map/ppermute | solution.py:144
  182.5 0.8 copy.32
  183.3 0.8 copy.31
  184.0 0.7 copy.30
  184.8 0.9 collective-permute-done
  185.7 0.8 maximum_convert_fusion
  (43 shorter events, 2.3 us)
Async XLA Ops:
  7.2 98.4 %all-gather.2.cloned.1.call-start = ((), (), s32[]{:S(2)}) async-start(), calls=%async_computation.4 | async-start | bytes 9437184 | tf_op jit(solution)/shard_map/all_gather | solution.py:91
  38.2 8.0 %copy-start = (bf16[1,128,2,128]{3,2,1,0:T(2,128)(2,1)S(1)}, bf16[1,128,2,128]{3,2,1,0:T(2,128)(2,1)}, u32[]{:S(2)}) copy-start(bf16[1,128,2,128]{3,2,1,0:T(2,128)(2,1)} %param.14) | copy-start | bytes 196612
  38.2 8.0 %copy-start.1 = (bf16[1,128,256]{2,1,0:T(8,128)(2,1)S(1)}, bf16[1,128,256]{2,1,0:T(8,128)(2,1)}, u32[]{:S(2)}) copy-start(bf16[1,128,256]{2,1,0:T(8,128)(2,1)} %param.13) | copy-start | bytes 196612
  38.2 8.8 %copy-start.2 = (bf16[1,128,256]{2,1,0:T(8,128)(2,1)S(1)}, bf16[1,128,256]{2,1,0:T(8,128)(2,1)}, u32[]{:S(2)}) copy-start(bf16[1,128,256]{2,1,0:T(8,128)(2,1)} %param.15) | copy-start | bytes 196612
  38.2 9.1 %copy-start.3 = (s32[1,128]{1,0:T(1,128)S(1)}, s32[1,128]{1,0:T(1,128)}, u32[]{:S(2)}) copy-start(s32[1,128]{1,0:T(1,128)} %param.17) | copy-start | bytes 1540
  38.2 9.2 %copy-start.4 = (s32[1,512]{1,0:T(1,128)S(1)}, s32[1,512]{1,0:T(1,128)}, u32[]{:S(2)}) copy-start(s32[1,512]{1,0:T(1,128)} %param.16) | copy-start | bytes 6148
  38.2 60.1 %all-to-all-start.1 = ((bf16[8,8,128,256]{3,2,1,0:T(8,128)(2,1)}), bf16[8,8,128,256]{3,2,1,0:T(8,128)(2,1)}, u32[]{:S(2)}, u32[]{:S(2)}) async-start(bf16[8,8,128,256]{3,2,1,0:T(8,128)(2,1)} %broadcast_in_dim.25), calls=%async_computation.1 | async-start | bytes 8388608 | tf_op jit(solution)/shard_map/all_to_all | solution.py:38
  45.4 113.3 %reduce-scatter.2.cloned.1.call-start = ((), (), s32[]{:S(2)}) async-start(), calls=%async_computation.5 | async-start | bytes 4718592 | tf_op jit(solution)/shard_map/reduce_scatter | solution.py:139
  113.1 3.4 %copy-start.5 = (bf16[512,8192]{1,0:T(8,128)(2,1)S(1)}, bf16[512,8192]{1,0:T(8,128)(2,1)}, u32[]{:S(2)}) copy-start(bf16[512,8192]{1,0:T(8,128)(2,1)} %all-gather.2.cloned.1.call-done) | copy-start | bytes 25165828
  158.7 20.7 %all-to-all-start.2 = ((bf16[8,128,256]{2,1,0:T(8,128)(2,1)}), bf16[8,128,256]{2,1,0:T(8,128)(2,1)S(1)}, u32[]{:S(2)}, u32[]{:S(2)}) async-start(bf16[8,128,256]{2,1,0:T(8,128)(2,1)} %bitcast.122), calls=%async_computation.3 | async-start | bytes 1048576 | tf_op jit(solution)/shard_map/all_to_all | solution.py:38
  179.5 6.2 %collective-permute-start = (bf16[128,256]{1,0:T(8,128)(2,1)S(1)}, bf16[128,256]{1,0:T(8,128)(2,1)S(1)}, u32[]{:S(2)}, u32[]{:S(2)}) collective-permute-start(bf16[128,256]{1,0:T(8,128)(2,1)S(1)} %reduce_sum.42), channel_id=1, source_target_pairs={{0,8},{8,0},{1,9},{9,1},{2,10},{10,2},{3,11},{11,3},{4,12},{12,4},... | collective-permute-start | bytes 196616 | tf_op jit(solution)/shard_map/ppermute | solution.py:144
Sparse Core Ops, SparseCore 0:
  12.3 58.8 all-gather.1
  121.4 37.2 reduce-scatter.1

commit v2 on v1

v2 whole, which is shorter than its diff:
```python
import jax
import jax.numpy as jnp
from jax import lax
from jax.experimental import pallas as pl
from jax.experimental.pallas import tpu as pltpu
from jax.sharding import Mesh
from jax.sharding import PartitionSpec as P

D = 8192
KVH = 8
HD = 128
QH = 16
STEPS = 1000
PREFIX = 512
ACT = 128
DP = ("dp_0", "dp_1")
DP_SEGMENT = ("dp_0", "dp_1", "segment")
EVERY = ("dp_0", "dp_1", "segment", "mp")
RING = 8
PART = D // RING // RING
COLUMNS = 2 * HD
WIDE = D // RING


EPS = 1e-06
NEGATIVE = -1e30
UNSEEN = 1 << 20


def rings(along_z_core):
    groups = []
    for x in range(4):
        for core in range(2):
            for other in range(RING):
                places = [
                    (k, other) if core == along_z_core else (other, k) for k in range(RING)
                ]
                groups.append([((z * RING + y) * 4 + x) * 2 + core for z, y in places])
    return groups


FIRST = rings(0)
SECOND = rings(1)


def exchange(parts, groups):
    return lax.all_to_all(
        parts, EVERY, split_axis=0, concat_axis=0, tiled=True, axis_index_groups=groups
    )


def shifted(array, groups, offset):
    pairs = [
        (group[k], group[(k + offset) % RING]) for group in groups for k in range(RING)
    ]
    return lax.ppermute(array, EVERY, pairs)


def around(array, groups):
    half = array.shape[0] // 2
    behind2 = shifted(array, groups, 2)
    ahead2 = shifted(array, groups, -2)
    behind1 = shifted(array, groups, 1)
    ahead1 = shifted(array, groups, -1)
    behind3 = shifted(behind2, groups, 1)
    ahead3 = shifted(ahead2, groups, -1)
    opposite_low = shifted(behind2[:half], groups, 2)
    opposite_high = shifted(ahead2[half:], groups, -2)
    return (
        array,
        ahead1,
        ahead2,
        ahead3,
        opposite_low,
        opposite_high,
        behind3,
        behind2,
        behind1,
    )


def dot(a, b):
    return jnp.dot(a, b, preferred_element_type=jnp.float32)


def dot_t(a, b):
    return lax.dot_general(a, b, (((1,), (1,)), ((), ())), preferred_element_type=jnp.float32)


def flipped(a):
    return jnp.transpose(a.astype(jnp.float32))


def attend_kernel(
    normed_ref,
    w0,
    w1,
    w2,
    w3,
    w4l,
    w4h,
    w5,
    w6,
    w7,
    query_ref,
    pair_ref,
    cot_ref,
    levels_ref,
    alevels_ref,
    flow_ref,
    out_ref,
    dq_ref,
    dpair_ref,
    term_ref,
    x_buf,
    w_buf,
    t_buf,
    acc,
    x_sem,
    w_sem,
    t_sem,
):
    core = lax.rem(lax.axis_index("mp"), 2)
    place_z = lax.axis_index("dp_0")
    place_y = lax.axis_index("dp_1") * 2 + lax.axis_index("segment")
    me = jnp.where(core == 0, place_y, place_z)
    half = RING // 2
    pieces = [
        (w0, 0, 0, RING),
        (w1, 1, 0, RING),
        (w2, 2, 0, RING),
        (w3, 3, 0, RING),
        (w4l, 4, 0, half),
        (w4h, 4, half, half),
        (w5, 5, 0, RING),
        (w6, 6, 0, RING),
        (w7, 7, 0, RING),
    ]

    def x_copy(j):
        block = pl.ds(j * WIDE, WIDE)
        return pltpu.make_async_copy(normed_ref.at[:, block], x_buf.at[:, block], x_sem.at[j])

    for k, (ref, ahead, start, size) in enumerate(pieces):
        spot = lax.rem(me + ahead, RING)

        @pl.when(core == 0)
        def _():
            pltpu.make_async_copy(
                ref, w_buf.at[pl.ds(start, size), spot], w_sem.at[k]
            ).start()

        @pl.when(core == 1)
        def _():
            pltpu.make_async_copy(
                ref, w_buf.at[spot, pl.ds(start, size)], w_sem.at[k]
            ).start()

    for j in range(RING):
        x_copy(j).start()
    for k, (ref, ahead, start, size) in enumerate(pieces):
        pltpu.make_async_copy(ref, w_buf.at[0, pl.ds(start, size)], w_sem.at[k]).wait()
    for j in range(RING):
        x_copy(j).wait()
        product = dot(x_buf[:, j * WIDE : (j + 1) * WIDE], w_buf[j].reshape(WIDE, COLUMNS))
        if j == 0:
            acc[...] = product
        else:
            acc[...] += product
    scale = HD ** (-0.5)
    keys = jnp.concatenate([acc[:, :HD].astype(jnp.bfloat16), pair_ref[:, :HD]], axis=0)
    values = jnp.concatenate([acc[:, HD:].astype(jnp.bfloat16), pair_ref[:, HD:]], axis=0)
    grads = (flow_ref[0] * cot_ref[...].astype(jnp.float32)).astype(jnp.bfloat16)
    query = jnp.concatenate([query_ref[:, :HD], query_ref[:, HD:]], axis=0)
    grad_out = jnp.concatenate([grads[:, :HD], grads[:, HD:]], axis=0)
    alevels = jnp.concatenate([alevels_ref[...], alevels_ref[...]], axis=0)
    visible = levels_ref[...] <= alevels
    masked = jnp.where(visible, dot_t(query, keys) * scale, NEGATIVE)
    top = jnp.max(masked, axis=-1, keepdims=True)
    expo = jnp.where(visible, jnp.exp(masked - top), 0.0)
    probs = expo / jnp.sum(expo, axis=-1, keepdims=True)
    probs_low = probs.astype(jnp.bfloat16)
    d_probs = dot_t(grad_out, values)
    delta = jnp.sum(probs * d_probs, axis=-1, keepdims=True)
    d_scores = (probs * (d_probs - delta)).astype(jnp.bfloat16)
    query_t = jnp.concatenate([flipped(query[:ACT]), flipped(query[ACT:])], axis=1)
    grad_out_t = jnp.concatenate([flipped(grad_out[:ACT]), flipped(grad_out[ACT:])], axis=1)
    d_keys_t = dot(query_t.astype(jnp.bfloat16), d_scores) * scale
    d_values_t = dot(grad_out_t.astype(jnp.bfloat16), probs_low)
    prefix_t = jnp.concatenate([d_keys_t[:, :PREFIX], d_values_t[:, :PREFIX]], axis=0).astype(
        jnp.bfloat16
    )
    for j in range(RING):
        block = dot(prefix_t, x_buf[:, j * WIDE : (j + 1) * WIDE]).astype(jnp.bfloat16)
        for k in range(RING):
            t_buf[j, k] = block[:, k * PART : (k + 1) * PART]

        @pl.when(core == 0)
        def _():
            pltpu.make_async_copy(t_buf.at[j], term_ref.at[:, j], t_sem.at[j]).start()

        @pl.when(core == 1)
        def _():
            pltpu.make_async_copy(t_buf.at[j], term_ref.at[j], t_sem.at[j]).start()

    out = dot(probs_low, values)
    d_query = dot(d_scores, keys) * scale
    out_ref[:, :HD] = out[:ACT].astype(jnp.bfloat16)
    out_ref[:, HD:] = out[ACT:].astype(jnp.bfloat16)
    dq_ref[:, :HD] = d_query[:ACT]
    dq_ref[:, HD:] = d_query[ACT:]
    dpair_ref[:, :HD] = flipped(d_keys_t[:, PREFIX:])
    dpair_ref[:, HD:] = flipped(d_values_t[:, PREFIX:])
    for j in range(RING):
        pltpu.make_async_copy(t_buf.at[j], term_ref.at[j], t_sem.at[j]).wait()


def attend(normed, weights, query, pair, cotangent, levels, alevels, flow):
    vmem = pl.BlockSpec(memory_space=pltpu.VMEM)
    anywhere = pl.BlockSpec(memory_space=pl.ANY)
    smem = pl.BlockSpec(memory_space=pltpu.SMEM)
    return pl.pallas_call(
        attend_kernel,
        out_shape=(
            jax.ShapeDtypeStruct((ACT, COLUMNS), jnp.bfloat16),
            jax.ShapeDtypeStruct((ACT, COLUMNS), jnp.float32),
            jax.ShapeDtypeStruct((ACT, COLUMNS), jnp.float32),
            jax.ShapeDtypeStruct((RING, RING, COLUMNS, PART), jnp.bfloat16),
        ),
        in_specs=[anywhere] * 10 + [vmem] * 5 + [smem],
        out_specs=(vmem, vmem, vmem, anywhere),
        scratch_shapes=[
            pltpu.VMEM((PREFIX, D), jnp.bfloat16),
            pltpu.VMEM((RING, RING, PART, COLUMNS), jnp.bfloat16),
            pltpu.VMEM((RING, RING, COLUMNS, PART), jnp.bfloat16),
            pltpu.VMEM((PREFIX, COLUMNS), jnp.float32),
            pltpu.SemaphoreType.DMA((RING,)),
            pltpu.SemaphoreType.DMA((9,)),
            pltpu.SemaphoreType.DMA((RING,)),
        ],
        compiler_params=pltpu.CompilerParams(vmem_limit_bytes=40 * 2**20),
        cost_estimate=pl.CostEstimate(
            flops=4 * PREFIX * D * COLUMNS, bytes_accessed=16 * 2**20, transcendentals=163840
        ),
    )(normed, *weights, query, pair, cotangent, levels, alevels, flow)


def shards(
    prefix_hidden,
    norm_gain,
    kv_weight,
    action_query,
    action_kv,
    out_cotangent,
    prefix_blocks,
    action_blocks,
    prefix_lengths,
    timesteps,
):
    wide = prefix_hidden[0].astype(jnp.float32)
    inverse = lax.rsqrt(jnp.mean(wide * wide, axis=-1, keepdims=True) + EPS)
    normed_local = (wide * inverse * norm_gain).astype(jnp.bfloat16)
    side = lax.axis_index("segment")
    local = kv_weight.reshape(2 * PART, COLUMNS)
    normed_local, local = lax.optimization_barrier((normed_local, local))
    normed = lax.all_gather(normed_local, "mp", axis=0, tiled=True)
    local = lax.dynamic_slice_in_dim(local, side * PART, PART, axis=0)
    line = exchange(jnp.broadcast_to(local, (RING, *local.shape)), FIRST)
    weights = around(line, SECOND)
    flow_weight = 0.5 + (timesteps.astype(jnp.float32) + 0.5) / STEPS
    positions = jnp.arange(PREFIX, dtype=jnp.int32)
    levels = jnp.where(positions[None, :] < prefix_lengths[0], prefix_blocks, UNSEEN)
    levels = jnp.concatenate([levels, action_blocks], axis=1)
    out, d_query, d_action, term = attend(
        normed,
        weights,
        action_query[0],
        action_kv[0].reshape(ACT, COLUMNS),
        out_cotangent[0],
        levels,
        action_blocks.reshape(ACT, 1),
        flow_weight,
    )
    ring_sum = lax.psum_scatter(
        term.reshape(RING * RING * COLUMNS, PART),
        EVERY,
        scatter_dimension=0,
        tiled=True,
        axis_index_groups=SECOND,
    )
    terms = exchange(ring_sum.reshape(RING, COLUMNS, PART), FIRST)
    own = jnp.sum(terms.astype(jnp.float32), axis=0).astype(jnp.bfloat16)
    theirs = lax.ppermute(own, "segment", [(0, 1), (1, 0)])
    low = jnp.where(side == 0, own, theirs)
    high = jnp.where(side == 0, theirs, own)
    weight_grad = jnp.concatenate([low, high], axis=1).astype(jnp.float32).T
    return (
        out[None],
        d_query[None],
        d_action.reshape(1, ACT, 2, HD),
        weight_grad.reshape(2 * PART, 2, HD),
    )


def solution(mesh):
    torus = Mesh(
        mesh.devices.reshape(8, 4, mesh.shape["segment"], mesh.shape["mp"]),
        ("dp_0", "dp_1", "segment", "mp"),
    )
    placed = (
        P(DP_SEGMENT, "mp", None),
        P(),
        P(DP, None, "mp"),
        P(DP_SEGMENT, None, "mp"),
        P(DP_SEGMENT, None, None, "mp"),
        P(DP_SEGMENT, None, "mp"),
        P(DP_SEGMENT, None),
        P(DP_SEGMENT, None),
        P(DP_SEGMENT),
        P(DP_SEGMENT),
    )
    return jax.shard_map(
        shards,
        mesh=torus,
        in_specs=placed,
        out_specs=(
            P(DP_SEGMENT, None, "mp"),
            P(DP_SEGMENT, None, "mp"),
            P(DP_SEGMENT, None, None, "mp"),
            P(DP, None, "mp"),
        ),
        check_vma=False,
    )
```

time: 194 us -> 175 us (0.902)
  waiting for transfers between devices: 102 us -> 54 us
  blocking collectives: 23.4 us -> 44.1 us
  starting transfers between devices: 17.7 us -> 34.4 us
  Pallas kernels: 0 us -> 13.9 us
  other arithmetic: 15.3 us -> 4.26 us
  matrix products: 11 us -> 0 us
    all_to_all x2 -> x0, waiting for transfers between devices: 63.4 us -> none  [exchange(): lax.all_to_all(parts, EVERY, split_axis=0, concat_axis=0, tiled=True, axi...]
    ppermute x0 -> x8, starting transfers between devices: none -> 31.3 us  [shifted(): return lax.ppermute(array, EVERY, pairs)]
    all_to_all x1 -> x2, blocking collectives: 23.4 us -> 44.1 us  [exchange(): lax.all_to_all(parts, EVERY, split_axis=0, concat_axis=0, tiled=True, axi...]
    all_to_all x2 -> x0, starting transfers between devices: 14.6 us -> none  [exchange(): lax.all_to_all(parts, EVERY, split_axis=0, concat_axis=0, tiled=True, axi...]
    pallas_call x0 -> x1, Pallas kernels: none -> 13.9 us  [attend(): pl.pallas_call(attend_kernel, out_shape=(jax.ShapeDtypeStruct((ACT, COLUM...]
    ppermute x0 -> x8, waiting for transfers between devices: none -> 11.2 us  [shifted(): return lax.ppermute(array, EVERY, pairs)]
    dot_general x8 -> x0, matrix products: 11 us -> none  [the longest x1 6.94 us: shards(): projected = jnp.dot(section, piece, preferred_element_type=jnp.float32)]
    select_n x2 -> x1, other arithmetic: 9.64 us -> 0.01 us  [shards(): jnp.where(positions[None, :] < prefix_lengths[0], prefix_blocks, UNSEEN)]
  transfers between devices with their start and end apart: 5 -> 11, of which waited for: 4 -> 6; matrix products, arithmetic and copies ran while one was open for 7% -> 1% of each run, Pallas kernels for 0% -> 0%
where the time goes in v2:
time: 175 us; the launch traced here: 174 us
  waiting for transfers between devices  54 us (31%)
  blocking collectives  44.1 us (25%)
  starting transfers between devices  34.4 us (20%)
  between operations  15.6 us (9%)
  Pallas kernels  13.9 us (8%)
  local copies, waits for them, and re-layouts  7.96 us (5%)
  other arithmetic  4.26 us (2%)
    all_to_all x2, blocking collectives, exchange(): lax.all_to_all(parts, EVERY, split_axis=0, concat_axis=0, tiled=True, axi...  44.1 us
    reduce_scatter x1, waiting for transfers between devices, shards(): lax.psum_scatter(term.reshape(RING * RING * COLUMNS, PART), EVERY, scatte...  40.4 us
    ppermute x8, starting transfers between devices, shifted(): return lax.ppermute(array, EVERY, pairs)  31.3 us
    pallas_call x1, Pallas kernels, attend(): pl.pallas_call(attend_kernel, out_shape=(jax.ShapeDtypeStruct((ACT, COLUM...  13.9 us
    ppermute x8, waiting for transfers between devices, shifted(): return lax.ppermute(array, EVERY, pairs)  11.2 us
    unnamed x23, local copies, waits for them, and re-layouts  7.04 us
  transfers between devices with their start and end apart: 11, of which 6 were waited for; matrix products, arithmetic and copies ran while one was open for 1% of the time, Pallas kernels for 0%

profile of v2, /device:TPU:2, one launch (start us, length us, event | category | flops | bytes accessed | tf_op | source)
XLA Modules:
  0.0 174.2 jit_solution(4848590185140569735)
XLA Ops:
  7.2 1.5 fusion
  8.8 0.9 copy.21
  9.7 2.6 %fusion.2 = bf16[64,8192]{1,0:T(8,128)(2,1)} fusion(bf16[1,64,8192]{2,1,0:T(8,128)(2,1)} %param.10, f32[8192]{0:T(1024)} %param.11, f32[64]{0:T(128)S(1)} %add_rsqrt_fusion), kind=kLoop, calls=%fused_computation.4 | loop fusion | flops 2097152 | bytes 2130176 | tf_op jit(solution)/shard_map/convert_element_type | solution.py:262
  12.5 23.4 %all_to_all.10.w0 = bf16[8,128,256]{2,1,0:T(8,128)(2,1)S(1)} all-to-all(bf16[8,128,256]{2,1,0:T(8,128)(2,1)S(1)} %broadcast_in_dim.16), channel_id=1, replica_groups={{0,64,128,192,256,320,384,448},{8,72,136,200,264,328,392,456},{16,80,14..., dimensions={0} | all-to-all | bytes 1048576 | tf_op jit(solution)/shard_map/all_to_all | solution.py:47
  35.9 4.5 %collective-permute-start.3 = (bf16[8,128,256]{2,1,0:T(8,128)(2,1)S(1)}, bf16[8,128,256]{2,1,0:T(8,128)(2,1)S(1)}, u32[]{:S(2)}, u32[]{:S(2)}) collective-permute-start(bf16[8,128,256]{2,1,0:T(8,128)(2,1)S(1)} %all_to_all.10.w0), channel_id=1, source_target_pairs={{0,16},{8,24},{16,32},{24,40},{32,48},{40,56},{48,0},{56,8},{64,80... | collective-permute-start | bytes 1572872 | tf_op jit(solution)/shard_map/ppermute | solution.py:56
  40.4 3.6 %collective-permute-start.1 = (bf16[8,128,256]{2,1,0:T(8,128)(2,1)S(1)}, bf16[8,128,256]{2,1,0:T(8,128)(2,1)S(1)}, u32[]{:S(2)}, u32[]{:S(2)}) collective-permute-start(bf16[8,128,256]{2,1,0:T(8,128)(2,1)S(1)} %all_to_all.10.w0), channel_id=1, source_target_pairs={{0,48},{8,56},{16,0},{24,8},{32,16},{40,24},{48,32},{56,40},{64,11... | collective-permute-start | bytes 1572872 | tf_op jit(solution)/shard_map/ppermute | solution.py:56
  44.0 3.4 %collective-permute-start.7 = (bf16[8,128,256]{2,1,0:T(8,128)(2,1)S(1)}, bf16[8,128,256]{2,1,0:T(8,128)(2,1)S(1)}, u32[]{:S(2)}, u32[]{:S(2)}) collective-permute-start(bf16[8,128,256]{2,1,0:T(8,128)(2,1)S(1)} %all_to_all.10.w0), channel_id=1, source_target_pairs={{0,8},{8,16},{16,24},{24,32},{32,40},{40,48},{48,56},{56,0},{64,72... | collective-permute-start | bytes 1572872 | tf_op jit(solution)/shard_map/ppermute | solution.py:56
  47.3 3.7 %collective-permute-start = (bf16[8,128,256]{2,1,0:T(8,128)(2,1)S(1)}, bf16[8,128,256]{2,1,0:T(8,128)(2,1)S(1)}, u32[]{:S(2)}, u32[]{:S(2)}) collective-permute-start(bf16[8,128,256]{2,1,0:T(8,128)(2,1)S(1)} %all_to_all.10.w0), channel_id=1, source_target_pairs={{0,56},{8,0},{16,8},{24,16},{32,24},{40,32},{48,40},{56,48},{64,12... | collective-permute-start | bytes 1572872 | tf_op jit(solution)/shard_map/ppermute | solution.py:56
  51.0 0.9 collective-permute-done.3.w6
  52.0 6.3 %collective-permute-start.6 = (bf16[8,128,256]{2,1,0:T(8,128)(2,1)S(1)}, bf16[8,128,256]{2,1,0:T(8,128)(2,1)S(1)}, u32[]{:S(2)}, u32[]{:S(2)}) collective-permute-start(bf16[8,128,256]{2,1,0:T(8,128)(2,1)S(1)} %collective-permute-done.3.w6), channel_id=1, source_target_pairs={{0,8},{8,16},{16,24},{24,32},{32,40},{40,48},{48,56},{56,0},{64,72... | collective-permute-start | bytes 1572872 | tf_op jit(solution)/shard_map/ppermute | solution.py:56
  59.0 1.9 %collective-permute-start.2 = (bf16[8,128,256]{2,1,0:T(8,128)(2,1)S(1)}, bf16[8,128,256]{2,1,0:T(8,128)(2,1)}, u32[]{:S(2)}, u32[]{:S(2)}) collective-permute-start(bf16[8,128,256]{2,1,0:T(8,128)(2,1)S(1)} %collective-permute-done.1.w2), channel_id=1, source_target_pairs={{0,56},{8,0},{16,8},{24,16},{32,24},{40,32},{48,40},{56,48},{64,12... | collective-permute-start | bytes 1572872 | tf_op jit(solution)/shard_map/ppermute | solution.py:56
  62.4 6.0 %collective-permute-start.4 = (bf16[4,128,256]{2,1,0:T(8,128)(2,1)S(1)}, bf16[4,128,256]{2,1,0:T(8,128)(2,1)S(1)}, u32[]{:S(2)}, u32[]{:S(2)}) collective-permute-start(bf16[4,128,256]{2,1,0:T(8,128)(2,1)S(1)} %slice.8), channel_id=1, source_target_pairs={{0,16},{8,24},{16,32},{24,40},{32,48},{40,56},{48,0},{56,8},{64,80... | collective-permute-start | bytes 786440 | tf_op jit(solution)/shard_map/ppermute | solution.py:56
  68.4 1.9 %collective-permute-start.5 = (bf16[4,128,256]{2,1,0:T(8,128)(2,1)S(1)}, bf16[4,128,256]{2,1,0:T(8,128)(2,1)S(1)}, u32[]{:S(2)}, u32[]{:S(2)}) collective-permute-start(bf16[4,128,256]{2,1,0:T(8,128)(2,1)S(1)} %slice.9), channel_id=1, source_target_pairs={{0,48},{8,56},{16,0},{24,8},{32,16},{40,24},{48,32},{56,40},{64,11... | collective-permute-start | bytes 786440 | tf_op jit(solution)/shard_map/ppermute | solution.py:56
  70.4 5.2 %collective-permute-done.4.w4l = bf16[4,128,256]{2,1,0:T(8,128)(2,1)S(1)} collective-permute-done((bf16[4,128,256]{2,1,0:T(8,128)(2,1)S(1)}, bf16[4,128,256]{2,1,0:T(8,128)(2,1)S(1)}, u32[]{:S(2)}, u32[]{:S(2)}) %collective-permute-start.4) | collective-permute-done | bytes 262176 | tf_op jit(solution)/shard_map/ppermute | solution.py:56
  76.3 4.4 %collective-permute-done.5.w4h = bf16[4,128,256]{2,1,0:T(8,128)(2,1)S(1)} collective-permute-done((bf16[4,128,256]{2,1,0:T(8,128)(2,1)S(1)}, bf16[4,128,256]{2,1,0:T(8,128)(2,1)S(1)}, u32[]{:S(2)}, u32[]{:S(2)}) %collective-permute-start.5) | collective-permute-done | bytes 262176 | tf_op jit(solution)/shard_map/ppermute | solution.py:56
  81.4 0.9 copy-done.2
  82.4 0.9 copy-done.4
  83.3 13.9 %shard_map.129 = (bf16[128,256]{1,0:T(8,128)(2,1)}, f32[128,256]{1,0:T(8,128)}, f32[128,256]{1,0:T(8,128)S(1)}, bf16[8,8,256,128]{3,2,1,0:T(8,128)(2,1)S(1)}) custom-call(bf16[512,8192]{1,0:T(8,128)(2,1)} %all-gather.2.cloned.1.call-done.normed_ref, bf16[8,128,256]{2,1,0:T(8,128)(2,1)S(1)} %all_to_all.10.w0, ...), custom_call_target="tpu_custom_call" | custom-call | flops 4294967296 | bytes 16777216 | tf_op jit(solution)/shard_map/pallas_call | solution.py:222
  97.2 1.9 %copy-done = bf16[8,8,256,128]{3,2,1,0:T(8,128)(2,1)} copy-done((bf16[8,8,256,128]{3,2,1,0:T(8,128)(2,1)}, bf16[8,8,256,128]{3,2,1,0:T(8,128)(2,1)S(1)}, u32[]{:S(2)}) %copy-start) | copy-done | bytes 4194328
  99.2 40.4 %reduce-scatter.2.cloned.1.call-done = bf16[2048,128]{1,0:T(8,128)(2,1)} async-done(((bf16[16384,128]{1,0:T(8,128)(2,1)}), bf16[2048,128]{1,0:T(8,128)(2,1)}) %reduce-scatter.2.cloned.1.call-update) | async-done | bytes 524304 | tf_op jit(solution)/shard_map/reduce_scatter | solution.py:284
  139.6 20.7 %all_to_all.11 = bf16[8,256,128]{2,1,0:T(8,128)(2,1)S(1)} all-to-all(bf16[8,256,128]{2,1,0:T(8,128)(2,1)} %bitcast.30), channel_id=1, replica_groups={{0,64,128,192,256,320,384,448},{8,72,136,200,264,328,392,456},{16,80,14..., dimensions={0} | all-to-all | bytes 1048576 | tf_op jit(solution)/shard_map/all_to_all | solution.py:47
  160.3 3.0 %collective-permute-start.8 = (bf16[256,128]{1,0:T(8,128)(2,1)S(1)}, bf16[256,128]{1,0:T(8,128)(2,1)S(1)}, u32[]{:S(2)}, u32[]{:S(2)}) collective-permute-start(bf16[256,128]{1,0:T(8,128)(2,1)S(1)} %reduce_sum.22), channel_id=1, source_target_pairs={{0,8},{8,0},{1,9},{9,1},{2,10},{10,2},{3,11},{11,3},{4,12},{12,4},... | collective-permute-start | bytes 196616 | tf_op jit(solution)/shard_map/ppermute | solution.py:293
  164.1 2.4 %collective-permute-done.8 = bf16[256,128]{1,0:T(8,128)(2,1)S(1)} collective-permute-done((bf16[256,128]{1,0:T(8,128)(2,1)S(1)}, bf16[256,128]{1,0:T(8,128)(2,1)S(1)}, u32[]{:S(2)}, u32[]{:S(2)}) %collective-permute-start.8) | collective-permute-done | bytes 65568 | tf_op jit(solution)/shard_map/ppermute | solution.py:293
  166.5 0.8 copy.16
  (40 shorter events, 3.3 us)
Async XLA Ops:
  7.2 74.2 %all-gather.2.cloned.1.call-start = ((), (), s32[]{:S(2)}) async-start(), calls=%async_computation.3 | async-start | bytes 9437184 | tf_op jit(solution)/shard_map/all_gather | solution.py:266
  9.7 52.5 %copy-start.7 = (bf16[1,128,2,128]{3,2,1,0:T(2,128)(2,1)S(1)}, bf16[1,128,2,128]{3,2,1,0:T(2,128)(2,1)}, u32[]{:S(2)}) copy-start(bf16[1,128,2,128]{3,2,1,0:T(2,128)(2,1)} %param.14) | copy-start | bytes 196612
  9.7 52.5 %copy-start.8 = (s32[1,128]{1,0:T(1,128)S(1)}, s32[1,128]{1,0:T(1,128)}, u32[]{:S(2)}) copy-start(s32[1,128]{1,0:T(1,128)} %param.17) | copy-start | bytes 1540
  12.3 58.0 %copy-start.9 = (s32[1,512]{1,0:T(1,128)S(1)}, s32[1,512]{1,0:T(1,128)}, u32[]{:S(2)}) copy-start(s32[1,512]{1,0:T(1,128)} %param.16) | copy-start | bytes 6148
  12.3 69.1 %copy-start.5 = (bf16[1,128,256]{2,1,0:T(8,128)(2,1)S(1)}, bf16[1,128,256]{2,1,0:T(8,128)(2,1)}, u32[]{:S(2)}) copy-start(bf16[1,128,256]{2,1,0:T(8,128)(2,1)} %param.13) | copy-start | bytes 196612
  12.3 69.1 %copy-start.6 = (bf16[1,128,256]{2,1,0:T(8,128)(2,1)S(1)}, bf16[1,128,256]{2,1,0:T(8,128)(2,1)}, u32[]{:S(2)}) copy-start(bf16[1,128,256]{2,1,0:T(8,128)(2,1)} %param.15) | copy-start | bytes 196612
  12.4 127.2 %reduce-scatter.2.cloned.1.call-start = ((), (), s32[]{:S(2)}) async-start(), calls=%async_computation.4 | async-start | bytes 4718592 | tf_op jit(solution)/shard_map/reduce_scatter | solution.py:284
  35.9 16.1 %collective-permute-start.3 = (bf16[8,128,256]{2,1,0:T(8,128)(2,1)S(1)}, bf16[8,128,256]{2,1,0:T(8,128)(2,1)S(1)}, u32[]{:S(2)}, u32[]{:S(2)}) collective-permute-start(bf16[8,128,256]{2,1,0:T(8,128)(2,1)S(1)} %all_to_all.10.w0), channel_id=1, source_target_pairs={{0,16},{8,24},{16,32},{24,40},{32,48},{40,56},{48,0},{56,8},{64,80... | collective-permute-start | bytes 1572872 | tf_op jit(solution)/shard_map/ppermute | solution.py:56
  40.4 18.6 %collective-permute-start.1 = (bf16[8,128,256]{2,1,0:T(8,128)(2,1)S(1)}, bf16[8,128,256]{2,1,0:T(8,128)(2,1)S(1)}, u32[]{:S(2)}, u32[]{:S(2)}) collective-permute-start(bf16[8,128,256]{2,1,0:T(8,128)(2,1)S(1)} %all_to_all.10.w0), channel_id=1, source_target_pairs={{0,48},{8,56},{16,0},{24,8},{32,16},{40,24},{48,32},{56,40},{64,11... | collective-permute-start | bytes 1572872 | tf_op jit(solution)/shard_map/ppermute | solution.py:56
  44.0 24.5 %collective-permute-start.7 = (bf16[8,128,256]{2,1,0:T(8,128)(2,1)S(1)}, bf16[8,128,256]{2,1,0:T(8,128)(2,1)S(1)}, u32[]{:S(2)}, u32[]{:S(2)}) collective-permute-start(bf16[8,128,256]{2,1,0:T(8,128)(2,1)S(1)} %all_to_all.10.w0), channel_id=1, source_target_pairs={{0,8},{8,16},{16,24},{24,32},{32,40},{40,48},{48,56},{56,0},{64,72... | collective-permute-start | bytes 1572872 | tf_op jit(solution)/shard_map/ppermute | solution.py:56
  47.3 23.1 %collective-permute-start = (bf16[8,128,256]{2,1,0:T(8,128)(2,1)S(1)}, bf16[8,128,256]{2,1,0:T(8,128)(2,1)S(1)}, u32[]{:S(2)}, u32[]{:S(2)}) collective-permute-start(bf16[8,128,256]{2,1,0:T(8,128)(2,1)S(1)} %all_to_all.10.w0), channel_id=1, source_target_pairs={{0,56},{8,0},{16,8},{24,16},{32,24},{40,32},{48,40},{56,48},{64,12... | collective-permute-start | bytes 1572872 | tf_op jit(solution)/shard_map/ppermute | solution.py:56
  52.0 29.4 %collective-permute-start.6 = (bf16[8,128,256]{2,1,0:T(8,128)(2,1)S(1)}, bf16[8,128,256]{2,1,0:T(8,128)(2,1)S(1)}, u32[]{:S(2)}, u32[]{:S(2)}) collective-permute-start(bf16[8,128,256]{2,1,0:T(8,128)(2,1)S(1)} %collective-permute-done.3.w6), channel_id=1, source_target_pairs={{0,8},{8,16},{16,24},{24,32},{32,40},{40,48},{48,56},{56,0},{64,72... | collective-permute-start | bytes 1572872 | tf_op jit(solution)/shard_map/ppermute | solution.py:56
  59.0 22.4 %collective-permute-start.2 = (bf16[8,128,256]{2,1,0:T(8,128)(2,1)S(1)}, bf16[8,128,256]{2,1,0:T(8,128)(2,1)}, u32[]{:S(2)}, u32[]{:S(2)}) collective-permute-start(bf16[8,128,256]{2,1,0:T(8,128)(2,1)S(1)} %collective-permute-done.1.w2), channel_id=1, source_target_pairs={{0,56},{8,0},{16,8},{24,16},{32,24},{40,32},{48,40},{56,48},{64,12... | collective-permute-start | bytes 1572872 | tf_op jit(solution)/shard_map/ppermute | solution.py:56
  62.4 13.2 %collective-permute-start.4 = (bf16[4,128,256]{2,1,0:T(8,128)(2,1)S(1)}, bf16[4,128,256]{2,1,0:T(8,128)(2,1)S(1)}, u32[]{:S(2)}, u32[]{:S(2)}) collective-permute-start(bf16[4,128,256]{2,1,0:T(8,128)(2,1)S(1)} %slice.8), channel_id=1, source_target_pairs={{0,16},{8,24},{16,32},{24,40},{32,48},{40,56},{48,0},{56,8},{64,80... | collective-permute-start | bytes 786440 | tf_op jit(solution)/shard_map/ppermute | solution.py:56
  68.4 12.3 %collective-permute-start.5 = (bf16[4,128,256]{2,1,0:T(8,128)(2,1)S(1)}, bf16[4,128,256]{2,1,0:T(8,128)(2,1)S(1)}, u32[]{:S(2)}, u32[]{:S(2)}) collective-permute-start(bf16[4,128,256]{2,1,0:T(8,128)(2,1)S(1)} %slice.9), channel_id=1, source_target_pairs={{0,48},{8,56},{16,0},{24,8},{32,16},{40,24},{48,32},{56,40},{64,11... | collective-permute-start | bytes 786440 | tf_op jit(solution)/shard_map/ppermute | solution.py:56
  75.6 0.7 copy-start.1
  80.7 0.7 copy-start.3
  81.4 1.0 copy-start.2
  82.4 0.9 copy-start.4
  97.2 2.0 %copy-start = (bf16[8,8,256,128]{3,2,1,0:T(8,128)(2,1)}, bf16[8,8,256,128]{3,2,1,0:T(8,128)(2,1)S(1)}, u32[]{:S(2)}) copy-start(bf16[8,8,256,128]{3,2,1,0:T(8,128)(2,1)S(1)} %get-tuple-element.15) | copy-start | bytes 12582916
  160.3 6.2 %collective-permute-start.8 = (bf16[256,128]{1,0:T(8,128)(2,1)S(1)}, bf16[256,128]{1,0:T(8,128)(2,1)S(1)}, u32[]{:S(2)}, u32[]{:S(2)}) collective-permute-start(bf16[256,128]{1,0:T(8,128)(2,1)S(1)} %reduce_sum.22), channel_id=1, source_target_pairs={{0,8},{8,0},{1,9},{9,1},{2,10},{10,2},{3,11},{11,3},{4,12},{12,4},... | collective-permute-start | bytes 196616 | tf_op jit(solution)/shard_map/ppermute | solution.py:293
Sparse Core Ops, SparseCore 0:
  12.5 58.8 all-gather.1
  99.3 40.1 reduce-scatter.1

commit v3 on v2

--- a/solution.py
+++ b/solution.py
@@ -20,6 +20,7 @@
 PART = D // RING // RING
 COLUMNS = 2 * HD
 WIDE = D // RING
+NORM_ROWS = 32
 
 
 EPS = 1e-06
@@ -56,27 +57,44 @@
     return lax.ppermute(array, EVERY, pairs)
 
 
-def around(array, groups):
-    half = array.shape[0] // 2
+def around(array, groups, place):
     behind2 = shifted(array, groups, 2)
     ahead2 = shifted(array, groups, -2)
     behind1 = shifted(array, groups, 1)
     ahead1 = shifted(array, groups, -1)
     behind3 = shifted(behind2, groups, 1)
     ahead3 = shifted(ahead2, groups, -1)
-    opposite_low = shifted(behind2[:half], groups, 2)
-    opposite_high = shifted(ahead2[half:], groups, -2)
-    return (
-        array,
-        ahead1,
-        ahead2,
-        ahead3,
-        opposite_low,
-        opposite_high,
-        behind3,
-        behind2,
-        behind1,
-    )
+    even = place % 2 == 0
+    onward = [
+        (group[k], group[(k + (2 if k % 2 == 0 else -2)) % RING])
+        for group in groups
+        for k in range(RING)
+    ]
+    opposite = lax.ppermute(jnp.where(even, behind2, ahead2), EVERY, onward)
+    return (array, ahead1, ahead2, ahead3, opposite, behind3, behind2, behind1)
+
+
+def norm_kernel(hidden_ref, gain_ref, out_ref):
+    wide = hidden_ref[0].astype(jnp.float32)
+    inverse = lax.rsqrt(jnp.mean(wide * wide, axis=-1, keepdims=True) + EPS)
+    out_ref[...] = (wide * inverse * gain_ref[...]).astype(jnp.bfloat16)
+
+
+def norm(hidden, gain):
+    tokens = hidden.shape[1]
+    return pl.pallas_call(
+        norm_kernel,
+        grid=(tokens // NORM_ROWS,),
+        out_shape=jax.ShapeDtypeStruct((tokens, D), jnp.bfloat16),
+        in_specs=[
+            pl.BlockSpec((1, NORM_ROWS, D), lambda i: (0, i, 0)),
+            pl.BlockSpec((1, D), lambda i: (0, 0)),
+        ],
+        out_specs=pl.BlockSpec((NORM_ROWS, D), lambda i: (i, 0)),
+        cost_estimate=pl.CostEstimate(
+            flops=4 * tokens * D, bytes_accessed=4 * tokens * D, transcendentals=tokens
+        ),
+    )(hidden, gain)
 
 
 def dot(a, b):
@@ -97,17 +115,14 @@
     w1,
     w2,
     w3,
-    w4l,
-    w4h,
+    w4,
     w5,
     w6,
     w7,
-    query_ref,
+    rows_ref,
     pair_ref,
-    cot_ref,
     levels_ref,
     alevels_ref,
-    flow_ref,
     out_ref,
     dq_ref,
     dpair_ref,
@@ -124,55 +139,40 @@
     place_z = lax.axis_index("dp_0")
     place_y = lax.axis_index("dp_1") * 2 + lax.axis_index("segment")
     me = jnp.where(core == 0, place_y, place_z)
-    half = RING // 2
-    pieces = [
-        (w0, 0, 0, RING),
-        (w1, 1, 0, RING),
-        (w2, 2, 0, RING),
-        (w3, 3, 0, RING),
-        (w4l, 4, 0, half),
-        (w4h, 4, half, half),
-        (w5, 5, 0, RING),
-        (w6, 6, 0, RING),
-        (w7, 7, 0, RING),
-    ]
+    pieces = (w0, w1, w2, w3, w4, w5, w6, w7)
 
     def x_copy(j):
         block = pl.ds(j * WIDE, WIDE)
         return pltpu.make_async_copy(normed_ref.at[:, block], x_buf.at[:, block], x_sem.at[j])
 
-    for k, (ref, ahead, start, size) in enumerate(pieces):
+    for ahead, piece in enumerate(pieces):
         spot = lax.rem(me + ahead, RING)
 
         @pl.when(core == 0)
         def _():
-            pltpu.make_async_copy(
-                ref, w_buf.at[pl.ds(start, size), spot], w_sem.at[k]
-            ).start()
+            pltpu.make_async_copy(piece, w_buf.at[:, spot], w_sem.at[ahead]).start()
 
         @pl.when(core == 1)
         def _():
-            pltpu.make_async_copy(
-                ref, w_buf.at[spot, pl.ds(start, size)], w_sem.at[k]
-            ).start()
+            pltpu.make_async_copy(piece, w_buf.at[spot], w_sem.at[ahead]).start()
 
     for j in range(RING):
         x_copy(j).start()
-    for k, (ref, ahead, start, size) in enumerate(pieces):
-        pltpu.make_async_copy(ref, w_buf.at[0, pl.ds(start, size)], w_sem.at[k]).wait()
-    for j in range(RING):
+    for ahead, piece in enumerate(pieces):
+        pltpu.make_async_copy(piece, w_buf.at[0], w_sem.at[ahead]).wait()
+    acc[...] = jnp.zeros_like(acc)
+
+    @pl.loop(0, RING)
+    def _(j):
         x_copy(j).wait()
-        product = dot(x_buf[:, j * WIDE : (j + 1) * WIDE], w_buf[j].reshape(WIDE, COLUMNS))
-        if j == 0:
-            acc[...] = product
-        else:
-            acc[...] += product
+        block = x_buf[:, pl.ds(pl.multiple_of(j * WIDE, WIDE), WIDE)]
+        acc[...] += dot(block, w_buf[j].reshape(WIDE, COLUMNS))
+
     scale = HD ** (-0.5)
     keys = jnp.concatenate([acc[:, :HD].astype(jnp.bfloat16), pair_ref[:, :HD]], axis=0)
     values = jnp.concatenate([acc[:, HD:].astype(jnp.bfloat16), pair_ref[:, HD:]], axis=0)
-    grads = (flow_ref[0] * cot_ref[...].astype(jnp.float32)).astype(jnp.bfloat16)
-    query = jnp.concatenate([query_ref[:, :HD], query_ref[:, HD:]], axis=0)
-    grad_out = jnp.concatenate([grads[:, :HD], grads[:, HD:]], axis=0)
+    query = jnp.concatenate([rows_ref[0, :, :HD], rows_ref[0, :, HD:]], axis=0)
+    grad_out = jnp.concatenate([rows_ref[1, :, :HD], rows_ref[1, :, HD:]], axis=0)
     alevels = jnp.concatenate([alevels_ref[...], alevels_ref[...]], axis=0)
     visible = levels_ref[...] <= alevels
     masked = jnp.where(visible, dot_t(query, keys) * scale, NEGATIVE)
@@ -215,10 +215,10 @@
         pltpu.make_async_copy(t_buf.at[j], term_ref.at[j], t_sem.at[j]).wait()
 
 
-def attend(normed, weights, query, pair, cotangent, levels, alevels, flow):
+def attend(normed, weights, rows, pair, levels, alevels):
     vmem = pl.BlockSpec(memory_space=pltpu.VMEM)
     anywhere = pl.BlockSpec(memory_space=pl.ANY)
-    smem = pl.BlockSpec(memory_space=pltpu.SMEM)
+    hbm = pl.BlockSpec(memory_space=pltpu.HBM)
     return pl.pallas_call(
         attend_kernel,
         out_shape=(
@@ -227,22 +227,22 @@
             jax.ShapeDtypeStruct((ACT, COLUMNS), jnp.float32),
             jax.ShapeDtypeStruct((RING, RING, COLUMNS, PART), jnp.bfloat16),
         ),
-        in_specs=[anywhere] * 10 + [vmem] * 5 + [smem],
-        out_specs=(vmem, vmem, vmem, anywhere),
+        in_specs=[hbm] + [anywhere] * 8 + [vmem] * 4,
+        out_specs=(vmem, vmem, vmem, hbm),
         scratch_shapes=[
             pltpu.VMEM((PREFIX, D), jnp.bfloat16),
             pltpu.VMEM((RING, RING, PART, COLUMNS), jnp.bfloat16),
             pltpu.VMEM((RING, RING, COLUMNS, PART), jnp.bfloat16),
             pltpu.VMEM((PREFIX, COLUMNS), jnp.float32),
             pltpu.SemaphoreType.DMA((RING,)),
-            pltpu.SemaphoreType.DMA((9,)),
+            pltpu.SemaphoreType.DMA((RING,)),
             pltpu.SemaphoreType.DMA((RING,)),
         ],
-        compiler_params=pltpu.CompilerParams(vmem_limit_bytes=40 * 2**20),
+        compiler_params=pltpu.CompilerParams(vmem_limit_bytes=48 * 2**20),
         cost_estimate=pl.CostEstimate(
             flops=4 * PREFIX * D * COLUMNS, bytes_accessed=16 * 2**20, transcendentals=163840
         ),
-    )(normed, *weights, query, pair, cotangent, levels, alevels, flow)
+    )(normed, *weights, rows, pair, levels, alevels)
 
 
 def shards(
@@ -257,29 +257,28 @@
     prefix_lengths,
     timesteps,
 ):
-    wide = prefix_hidden[0].astype(jnp.float32)
-    inverse = lax.rsqrt(jnp.mean(wide * wide, axis=-1, keepdims=True) + EPS)
-    normed_local = (wide * inverse * norm_gain).astype(jnp.bfloat16)
+    normed_local = norm(prefix_hidden, norm_gain.reshape(1, D))
     side = lax.axis_index("segment")
     local = kv_weight.reshape(2 * PART, COLUMNS)
     normed_local, local = lax.optimization_barrier((normed_local, local))
     normed = lax.all_gather(normed_local, "mp", axis=0, tiled=True)
     local = lax.dynamic_slice_in_dim(local, side * PART, PART, axis=0)
     line = exchange(jnp.broadcast_to(local, (RING, *local.shape)), FIRST)
-    weights = around(line, SECOND)
-    flow_weight = 0.5 + (timesteps.astype(jnp.float32) + 0.5) / STEPS
+    core = lax.axis_index("mp") % 2
+    place = jnp.where(core == 0, lax.axis_index("dp_1") * 2 + side, lax.axis_index("dp_0"))
+    weights = around(line, SECOND, place)
+    flow_weight = 0.5 + (timesteps[0].astype(jnp.float32) + 0.5) / STEPS
+    grad_out = (flow_weight * out_cotangent[0].astype(jnp.float32)).astype(jnp.bfloat16)
     positions = jnp.arange(PREFIX, dtype=jnp.int32)
     levels = jnp.where(positions[None, :] < prefix_lengths[0], prefix_blocks, UNSEEN)
     levels = jnp.concatenate([levels, action_blocks], axis=1)
     out, d_query, d_action, term = attend(
         normed,
         weights,
-        action_query[0],
+        jnp.stack([action_query[0], grad_out]),
         action_kv[0].reshape(ACT, COLUMNS),
-        out_cotangent[0],
         levels,
         action_blocks.reshape(ACT, 1),
-        flow_weight,
     )
     ring_sum = lax.psum_scatter(
         term.reshape(RING * RING * COLUMNS, PART),

time: 175 us -> 164 us (0.937)
  the two profiles are of different devices: /device:TPU:2 before, /device:TPU:4 now
where the time goes in v3:
time: 164 us; the launch traced here: 163 us
  waiting for transfers between devices  51.7 us (32%)
  blocking collectives  44.1 us (27%)
  starting transfers between devices  31.2 us (19%)
  between operations  15.5 us (9%)
  Pallas kernels  12.6 us (8%)
  local copies, waits for them, and re-layouts  4.15 us (3%)
  other arithmetic  4.02 us (2%)
    all_to_all x2, blocking collectives, exchange(): lax.all_to_all(parts, EVERY, split_axis=0, concat_axis=0, tiled=True, axi...  44.1 us
    reduce_scatter x1, waiting for transfers between devices, shards(): lax.psum_scatter(term.reshape(RING * RING * COLUMNS, PART), EVERY, scatte...  40.6 us
    ppermute x6, starting transfers between devices, shifted(): return lax.ppermute(array, EVERY, pairs)  22.2 us
    pallas_call x1, Pallas kernels, attend(): pl.pallas_call(attend_kernel, out_shape=(jax.ShapeDtypeStruct((ACT, COLUM...  10 us
    ppermute x6, waiting for transfers between devices, shifted(): return lax.ppermute(array, EVERY, pairs)  8.57 us
    ppermute x1, starting transfers between devices, around(): opposite = lax.ppermute(jnp.where(even, behind2, ahead2), EVERY, onward)  6.02 us
  transfers between devices with their start and end apart: 10, of which 6 were waited for; matrix products, arithmetic and copies ran while one was open for 4% of the time, Pallas kernels for 0%

profile of v3, /device:TPU:4, one launch (start us, length us, event | category | flops | bytes accessed | tf_op | source)
XLA Modules:
  0.0 163.3 jit_solution(17523995950369683422)
XLA Ops:
  7.2 0.9 copy.21
  8.1 2.6 %shard_map.129 = bf16[64,8192]{1,0:T(8,128)(2,1)} custom-call(bf16[1,64,8192]{2,1,0:T(8,128)(2,1)} %hidden_ref.1, f32[1,8192]{1,0:T(1,128)} %bitcast.28), custom_call_target="tpu_custom_call" | custom-call | flops 2097152 | bytes 2097152 | tf_op jit(solution)/shard_map/pallas_call | solution.py:85
  10.9 23.4 %all_to_all.10.w0 = bf16[8,128,256]{2,1,0:T(8,128)(2,1)S(1)} all-to-all(bf16[8,128,256]{2,1,0:T(8,128)(2,1)S(1)} %broadcast_in_dim.14), channel_id=1, replica_groups={{0,64,128,192,256,320,384,448},{8,72,136,200,264,328,392,456},{16,80,14..., dimensions={0} | all-to-all | bytes 1048576 | tf_op jit(solution)/shard_map/all_to_all | solution.py:48
  34.3 4.5 %collective-permute-start.3 = (bf16[8,128,256]{2,1,0:T(8,128)(2,1)S(1)}, bf16[8,128,256]{2,1,0:T(8,128)(2,1)S(1)}, u32[]{:S(2)}, u32[]{:S(2)}) collective-permute-start(bf16[8,128,256]{2,1,0:T(8,128)(2,1)S(1)} %all_to_all.10.w0), channel_id=1, source_target_pairs={{0,16},{8,24},{16,32},{24,40},{32,48},{40,56},{48,0},{56,8},{64,80... | collective-permute-start | bytes 1572872 | tf_op jit(solution)/shard_map/ppermute | solution.py:57
  38.8 3.6 %collective-permute-start.1 = (bf16[8,128,256]{2,1,0:T(8,128)(2,1)S(1)}, bf16[8,128,256]{2,1,0:T(8,128)(2,1)S(1)}, u32[]{:S(2)}, u32[]{:S(2)}) collective-permute-start(bf16[8,128,256]{2,1,0:T(8,128)(2,1)S(1)} %all_to_all.10.w0), channel_id=1, source_target_pairs={{0,48},{8,56},{16,0},{24,8},{32,16},{40,24},{48,32},{56,40},{64,11... | collective-permute-start | bytes 1572872 | tf_op jit(solution)/shard_map/ppermute | solution.py:57
  43.0 3.4 %collective-permute-start.6 = (bf16[8,128,256]{2,1,0:T(8,128)(2,1)S(1)}, bf16[8,128,256]{2,1,0:T(8,128)(2,1)S(1)}, u32[]{:S(2)}, u32[]{:S(2)}) collective-permute-start(bf16[8,128,256]{2,1,0:T(8,128)(2,1)S(1)} %all_to_all.10.w0), channel_id=1, source_target_pairs={{0,8},{8,16},{16,24},{24,32},{32,40},{40,48},{48,56},{56,0},{64,72... | collective-permute-start | bytes 1572872 | tf_op jit(solution)/shard_map/ppermute | solution.py:57
  46.4 3.7 %collective-permute-start = (bf16[8,128,256]{2,1,0:T(8,128)(2,1)S(1)}, bf16[8,128,256]{2,1,0:T(8,128)(2,1)S(1)}, u32[]{:S(2)}, u32[]{:S(2)}) collective-permute-start(bf16[8,128,256]{2,1,0:T(8,128)(2,1)S(1)} %all_to_all.10.w0), channel_id=1, source_target_pairs={{0,56},{8,0},{16,8},{24,16},{32,24},{40,32},{48,40},{56,48},{64,12... | collective-permute-start | bytes 1572872 | tf_op jit(solution)/shard_map/ppermute | solution.py:57
  50.4 7.0 %collective-permute-done.1.w2 = bf16[8,128,256]{2,1,0:T(8,128)(2,1)S(1)} collective-permute-done((bf16[8,128,256]{2,1,0:T(8,128)(2,1)S(1)}, bf16[8,128,256]{2,1,0:T(8,128)(2,1)S(1)}, u32[]{:S(2)}, u32[]{:S(2)}) %collective-permute-start.1) | collective-permute-done | bytes 524320 | tf_op jit(solution)/shard_map/ppermute | solution.py:57
  57.3 0.9 broadcast_select_fusion
  58.2 6.0 %collective-permute-start.4 = (bf16[8,128,256]{2,1,0:T(8,128)(2,1)}, bf16[8,128,256]{2,1,0:T(8,128)(2,1)S(1)}, u32[]{:S(2)}, u32[]{:S(2)}) collective-permute-start(bf16[8,128,256]{2,1,0:T(8,128)(2,1)} %broadcast_select_fusion), channel_id=1, source_target_pairs={{0,16},{8,56},{16,32},{24,8},{32,48},{40,24},{48,0},{56,40},{64,80... | collective-permute-start | bytes 1572872 | tf_op jit(solution)/shard_map/ppermute | solution.py:73
  64.2 1.9 %collective-permute-start.5 = (bf16[8,128,256]{2,1,0:T(8,128)(2,1)S(1)}, bf16[8,128,256]{2,1,0:T(8,128)(2,1)}, u32[]{:S(2)}, u32[]{:S(2)}) collective-permute-start(bf16[8,128,256]{2,1,0:T(8,128)(2,1)S(1)} %collective-permute-done.3.w6), channel_id=1, source_target_pairs={{0,8},{8,16},{16,24},{24,32},{32,40},{40,48},{48,56},{56,0},{64,72... | collective-permute-start | bytes 1572872 | tf_op jit(solution)/shard_map/ppermute | solution.py:57
  66.2 5.1 %collective-permute-start.2 = (bf16[8,128,256]{2,1,0:T(8,128)(2,1)S(1)}, bf16[8,128,256]{2,1,0:T(8,128)(2,1)}, u32[]{:S(2)}, u32[]{:S(2)}) collective-permute-start(bf16[8,128,256]{2,1,0:T(8,128)(2,1)S(1)} %collective-permute-done.1.w2), channel_id=1, source_target_pairs={{0,56},{8,0},{16,8},{24,16},{32,24},{40,32},{48,40},{56,48},{64,12... | collective-permute-start | bytes 1572872 | tf_op jit(solution)/shard_map/ppermute | solution.py:57
  71.3 0.7 compare_select_fusion
  72.6 0.9 copy.22
  73.5 0.8 copy.15.alevels_ref
  74.9 0.9 multiply_convert_fusion
  75.8 0.9 pad_maximum_fusion.rows_ref
  78.0 10.0 %shard_map.130 = (bf16[128,256]{1,0:T(8,128)(2,1)}, f32[128,256]{1,0:T(8,128)}, f32[128,256]{1,0:T(8,128)S(1)}, bf16[8,8,256,128]{3,2,1,0:T(8,128)(2,1)}) custom-call(bf16[512,8192]{1,0:T(8,128)(2,1)} %all-gather.2.cloned.1.call-done.normed_ref, bf16[8,128,256]{2,1,0:T(8,128)(2,1)S(1)} %all_to_all.10.w0, bf16[8,128,256]{2,1,0:T(8,128)(2,1)S(1)} %collective-permute-done.w1, ...), custom_call_target="tpu_custom_call" | custom-call | flops 4294967296 | bytes 16777216 | tf_op jit(solution)/shard_map/pallas_call | solution.py:222
  88.0 40.6 %reduce-scatter.2.cloned.1.call-done = bf16[2048,128]{1,0:T(8,128)(2,1)} async-done(((bf16[16384,128]{1,0:T(8,128)(2,1)}), bf16[2048,128]{1,0:T(8,128)(2,1)}) %reduce-scatter.2.cloned.1.call-update) | async-done | bytes 524304 | tf_op jit(solution)/shard_map/reduce_scatter | solution.py:283
  128.6 20.7 %all_to_all.11 = bf16[8,256,128]{2,1,0:T(8,128)(2,1)S(1)} all-to-all(bf16[8,256,128]{2,1,0:T(8,128)(2,1)} %bitcast.24), channel_id=1, replica_groups={{0,64,128,192,256,320,384,448},{8,72,136,200,264,328,392,456},{16,80,14..., dimensions={0} | all-to-all | bytes 1048576 | tf_op jit(solution)/shard_map/all_to_all | solution.py:48
  149.4 3.0 %collective-permute-start.7 = (bf16[256,128]{1,0:T(8,128)(2,1)S(1)}, bf16[256,128]{1,0:T(8,128)(2,1)S(1)}, u32[]{:S(2)}, u32[]{:S(2)}) collective-permute-start(bf16[256,128]{1,0:T(8,128)(2,1)S(1)} %reduce_sum.12), channel_id=1, source_target_pairs={{0,8},{8,0},{1,9},{9,1},{2,10},{10,2},{3,11},{11,3},{4,12},{12,4},... | collective-permute-start | bytes 196616 | tf_op jit(solution)/shard_map/ppermute | solution.py:292
  152.4 0.7 reshape.50
  153.1 2.5 %collective-permute-done.7 = bf16[256,128]{1,0:T(8,128)(2,1)S(1)} collective-permute-done((bf16[256,128]{1,0:T(8,128)(2,1)S(1)}, bf16[256,128]{1,0:T(8,128)(2,1)S(1)}, u32[]{:S(2)}, u32[]{:S(2)}) %collective-permute-start.7) | collective-permute-done | bytes 65568 | tf_op jit(solution)/shard_map/ppermute | solution.py:292
  155.7 0.8 copy.16
  (17 shorter events, 2.5 us)
Async XLA Ops:
  7.2 70.8 %all-gather.2.cloned.1.call-start = ((), (), s32[]{:S(2)}) async-start(), calls=%async_computation.3 | async-start | bytes 9437184 | tf_op jit(solution)/shard_map/all_gather | solution.py:264
  10.7 117.9 %reduce-scatter.2.cloned.1.call-start = ((), (), s32[]{:S(2)}) async-start(), calls=%async_computation.4 | async-start | bytes 4718592 | tf_op jit(solution)/shard_map/reduce_scatter | solution.py:283
  34.3 16.1 %collective-permute-start.3 = (bf16[8,128,256]{2,1,0:T(8,128)(2,1)S(1)}, bf16[8,128,256]{2,1,0:T(8,128)(2,1)S(1)}, u32[]{:S(2)}, u32[]{:S(2)}) collective-permute-start(bf16[8,128,256]{2,1,0:T(8,128)(2,1)S(1)} %all_to_all.10.w0), channel_id=1, source_target_pairs={{0,16},{8,24},{16,32},{24,40},{32,48},{40,56},{48,0},{56,8},{64,80... | collective-permute-start | bytes 1572872 | tf_op jit(solution)/shard_map/ppermute | solution.py:57
  38.8 18.6 %collective-permute-start.1 = (bf16[8,128,256]{2,1,0:T(8,128)(2,1)S(1)}, bf16[8,128,256]{2,1,0:T(8,128)(2,1)S(1)}, u32[]{:S(2)}, u32[]{:S(2)}) collective-permute-start(bf16[8,128,256]{2,1,0:T(8,128)(2,1)S(1)} %all_to_all.10.w0), channel_id=1, source_target_pairs={{0,48},{8,56},{16,0},{24,8},{32,16},{40,24},{48,32},{56,40},{64,11... | collective-permute-start | bytes 1572872 | tf_op jit(solution)/shard_map/ppermute | solution.py:57
  43.0 33.6 %collective-permute-start.6 = (bf16[8,128,256]{2,1,0:T(8,128)(2,1)S(1)}, bf16[8,128,256]{2,1,0:T(8,128)(2,1)S(1)}, u32[]{:S(2)}, u32[]{:S(2)}) collective-permute-start(bf16[8,128,256]{2,1,0:T(8,128)(2,1)S(1)} %all_to_all.10.w0), channel_id=1, source_target_pairs={{0,8},{8,16},{16,24},{24,32},{32,40},{40,48},{48,56},{56,0},{64,72... | collective-permute-start | bytes 1572872 | tf_op jit(solution)/shard_map/ppermute | solution.py:57
  46.4 30.3 %collective-permute-start = (bf16[8,128,256]{2,1,0:T(8,128)(2,1)S(1)}, bf16[8,128,256]{2,1,0:T(8,128)(2,1)S(1)}, u32[]{:S(2)}, u32[]{:S(2)}) collective-permute-start(bf16[8,128,256]{2,1,0:T(8,128)(2,1)S(1)} %all_to_all.10.w0), channel_id=1, source_target_pairs={{0,56},{8,0},{16,8},{24,16},{32,24},{40,32},{48,40},{56,48},{64,12... | collective-permute-start | bytes 1572872 | tf_op jit(solution)/shard_map/ppermute | solution.py:57
  58.2 19.1 %collective-permute-start.4 = (bf16[8,128,256]{2,1,0:T(8,128)(2,1)}, bf16[8,128,256]{2,1,0:T(8,128)(2,1)S(1)}, u32[]{:S(2)}, u32[]{:S(2)}) collective-permute-start(bf16[8,128,256]{2,1,0:T(8,128)(2,1)} %broadcast_select_fusion), channel_id=1, source_target_pairs={{0,16},{8,56},{16,32},{24,8},{32,48},{40,24},{48,0},{56,40},{64,80... | collective-permute-start | bytes 1572872 | tf_op jit(solution)/shard_map/ppermute | solution.py:73
  64.2 13.1 %collective-permute-start.5 = (bf16[8,128,256]{2,1,0:T(8,128)(2,1)S(1)}, bf16[8,128,256]{2,1,0:T(8,128)(2,1)}, u32[]{:S(2)}, u32[]{:S(2)}) collective-permute-start(bf16[8,128,256]{2,1,0:T(8,128)(2,1)S(1)} %collective-permute-done.3.w6), channel_id=1, source_target_pairs={{0,8},{8,16},{16,24},{24,32},{32,40},{40,48},{48,56},{56,0},{64,72... | collective-permute-start | bytes 1572872 | tf_op jit(solution)/shard_map/ppermute | solution.py:57
  66.2 11.8 %collective-permute-start.2 = (bf16[8,128,256]{2,1,0:T(8,128)(2,1)S(1)}, bf16[8,128,256]{2,1,0:T(8,128)(2,1)}, u32[]{:S(2)}, u32[]{:S(2)}) collective-permute-start(bf16[8,128,256]{2,1,0:T(8,128)(2,1)S(1)} %collective-permute-done.1.w2), channel_id=1, source_target_pairs={{0,56},{8,0},{16,8},{24,16},{32,24},{40,32},{48,40},{56,48},{64,12... | collective-permute-start | bytes 1572872 | tf_op jit(solution)/shard_map/ppermute | solution.py:57
  149.4 6.2 %collective-permute-start.7 = (bf16[256,128]{1,0:T(8,128)(2,1)S(1)}, bf16[256,128]{1,0:T(8,128)(2,1)S(1)}, u32[]{:S(2)}, u32[]{:S(2)}) collective-permute-start(bf16[256,128]{1,0:T(8,128)(2,1)S(1)} %reduce_sum.12), channel_id=1, source_target_pairs={{0,8},{8,0},{1,9},{9,1},{2,10},{10,2},{3,11},{11,3},{4,12},{12,4},... | collective-permute-start | bytes 196616 | tf_op jit(solution)/shard_map/ppermute | solution.py:292
Sparse Core Ops, SparseCore 0:
  10.9 58.5 all-gather.1
  88.1 40.4 reduce-scatter.1

commit v4 on v3

--- a/solution.py
+++ b/solution.py
@@ -259,10 +259,9 @@
 ):
     normed_local = norm(prefix_hidden, norm_gain.reshape(1, D))
     side = lax.axis_index("segment")
-    local = kv_weight.reshape(2 * PART, COLUMNS)
-    normed_local, local = lax.optimization_barrier((normed_local, local))
+    normed_local, local = lax.optimization_barrier((normed_local, kv_weight))
     normed = lax.all_gather(normed_local, "mp", axis=0, tiled=True)
-    local = lax.dynamic_slice_in_dim(local, side * PART, PART, axis=0)
+    local = lax.dynamic_slice_in_dim(local, side * PART, PART, axis=0).reshape(PART, COLUMNS)
     line = exchange(jnp.broadcast_to(local, (RING, *local.shape)), FIRST)
     core = lax.axis_index("mp") % 2
     place = jnp.where(core == 0, lax.axis_index("dp_1") * 2 + side, lax.axis_index("dp_0"))

time: 164 us -> 163 us (level)
  the two profiles are of different devices: /device:TPU:4 before, /device:TPU:2 now
where the time goes in v4:
time: 163 us
  waiting for transfers between devices  51.6 us (32%)
  blocking collectives  44.1 us (27%)
  starting transfers between devices  31.3 us (19%)
  between operations  15.5 us (10%)
  Pallas kernels  12.7 us (8%)
  other arithmetic  4.03 us (2%)
  local copies, waits for them, and re-layouts  3.28 us (2%)
    all_to_all x2, blocking collectives, exchange(): lax.all_to_all(parts, EVERY, split_axis=0, concat_axis=0, tiled=True, axi...  44.1 us
    reduce_scatter x1, waiting for transfers between devices, shards(): lax.psum_scatter(term.reshape(RING * RING * COLUMNS, PART), EVERY, scatte...  40.6 us
    ppermute x6, starting transfers between devices, shifted(): return lax.ppermute(array, EVERY, pairs)  22.2 us
    pallas_call x1, Pallas kernels, attend(): pl.pallas_call(attend_kernel, out_shape=(jax.ShapeDtypeStruct((ACT, COLUM...  10.2 us
    ppermute x6, waiting for transfers between devices, shifted(): return lax.ppermute(array, EVERY, pairs)  8.57 us
    ppermute x1, starting transfers between devices, around(): opposite = lax.ppermute(jnp.where(even, behind2, ahead2), EVERY, onward)  6.02 us
  transfers between devices with their start and end apart: 10, of which 6 were waited for; matrix products, arithmetic and copies ran while one was open for 4% of the time, Pallas kernels for 0%

profile of v4, /device:TPU:2, one launch (start us, length us, event | category | flops | bytes accessed | tf_op | source)
XLA Modules:
  0.0 162.6 jit_solution(14499715233550120279)
XLA Ops:
  7.2 2.6 %shard_map.129 = bf16[64,8192]{1,0:T(8,128)(2,1)} custom-call(bf16[1,64,8192]{2,1,0:T(8,128)(2,1)} %hidden_ref.1, f32[1,8192]{1,0:T(1,128)} %bitcast.28), custom_call_target="tpu_custom_call" | custom-call | flops 2097152 | bytes 2097152 | tf_op jit(solution)/shard_map/pallas_call | solution.py:85
  10.0 23.4 %all_to_all.10.w0 = bf16[8,128,256]{2,1,0:T(8,128)(2,1)S(1)} all-to-all(bf16[8,128,256]{2,1,0:T(8,128)(2,1)S(1)} %broadcast_in_dim.14), channel_id=1, replica_groups={{0,64,128,192,256,320,384,448},{8,72,136,200,264,328,392,456},{16,80,14..., dimensions={0} | all-to-all | bytes 1048576 | tf_op jit(solution)/shard_map/all_to_all | solution.py:48
  33.4 4.5 %collective-permute-start.3 = (bf16[8,128,256]{2,1,0:T(8,128)(2,1)S(1)}, bf16[8,128,256]{2,1,0:T(8,128)(2,1)S(1)}, u32[]{:S(2)}, u32[]{:S(2)}) collective-permute-start(bf16[8,128,256]{2,1,0:T(8,128)(2,1)S(1)} %all_to_all.10.w0), channel_id=1, source_target_pairs={{0,16},{8,24},{16,32},{24,40},{32,48},{40,56},{48,0},{56,8},{64,80... | collective-permute-start | bytes 1572872 | tf_op jit(solution)/shard_map/ppermute | solution.py:57
  37.9 3.6 %collective-permute-start.1 = (bf16[8,128,256]{2,1,0:T(8,128)(2,1)S(1)}, bf16[8,128,256]{2,1,0:T(8,128)(2,1)S(1)}, u32[]{:S(2)}, u32[]{:S(2)}) collective-permute-start(bf16[8,128,256]{2,1,0:T(8,128)(2,1)S(1)} %all_to_all.10.w0), channel_id=1, source_target_pairs={{0,48},{8,56},{16,0},{24,8},{32,16},{40,24},{48,32},{56,40},{64,11... | collective-permute-start | bytes 1572872 | tf_op jit(solution)/shard_map/ppermute | solution.py:57
  42.2 3.4 %collective-permute-start.6 = (bf16[8,128,256]{2,1,0:T(8,128)(2,1)S(1)}, bf16[8,128,256]{2,1,0:T(8,128)(2,1)S(1)}, u32[]{:S(2)}, u32[]{:S(2)}) collective-permute-start(bf16[8,128,256]{2,1,0:T(8,128)(2,1)S(1)} %all_to_all.10.w0), channel_id=1, source_target_pairs={{0,8},{8,16},{16,24},{24,32},{32,40},{40,48},{48,56},{56,0},{64,72... | collective-permute-start | bytes 1572872 | tf_op jit(solution)/shard_map/ppermute | solution.py:57
  45.5 3.7 %collective-permute-start = (bf16[8,128,256]{2,1,0:T(8,128)(2,1)S(1)}, bf16[8,128,256]{2,1,0:T(8,128)(2,1)S(1)}, u32[]{:S(2)}, u32[]{:S(2)}) collective-permute-start(bf16[8,128,256]{2,1,0:T(8,128)(2,1)S(1)} %all_to_all.10.w0), channel_id=1, source_target_pairs={{0,56},{8,0},{16,8},{24,16},{32,24},{40,32},{48,40},{56,48},{64,12... | collective-permute-start | bytes 1572872 | tf_op jit(solution)/shard_map/ppermute | solution.py:57
  49.5 7.0 %collective-permute-done.1.w2 = bf16[8,128,256]{2,1,0:T(8,128)(2,1)S(1)} collective-permute-done((bf16[8,128,256]{2,1,0:T(8,128)(2,1)S(1)}, bf16[8,128,256]{2,1,0:T(8,128)(2,1)S(1)}, u32[]{:S(2)}, u32[]{:S(2)}) %collective-permute-start.1) | collective-permute-done | bytes 524320 | tf_op jit(solution)/shard_map/ppermute | solution.py:57
  56.5 0.9 broadcast_select_fusion
  57.3 6.0 %collective-permute-start.4 = (bf16[8,128,256]{2,1,0:T(8,128)(2,1)}, bf16[8,128,256]{2,1,0:T(8,128)(2,1)}, u32[]{:S(2)}, u32[]{:S(2)}) collective-permute-start(bf16[8,128,256]{2,1,0:T(8,128)(2,1)} %broadcast_select_fusion), channel_id=1, source_target_pairs={{0,16},{8,56},{16,32},{24,8},{32,48},{40,24},{48,0},{56,40},{64,80... | collective-permute-start | bytes 1572872 | tf_op jit(solution)/shard_map/ppermute | solution.py:73
  63.4 1.9 %collective-permute-start.5 = (bf16[8,128,256]{2,1,0:T(8,128)(2,1)S(1)}, bf16[8,128,256]{2,1,0:T(8,128)(2,1)}, u32[]{:S(2)}, u32[]{:S(2)}) collective-permute-start(bf16[8,128,256]{2,1,0:T(8,128)(2,1)S(1)} %collective-permute-done.3.w6), channel_id=1, source_target_pairs={{0,8},{8,16},{16,24},{24,32},{32,40},{40,48},{48,56},{56,0},{64,72... | collective-permute-start | bytes 1572872 | tf_op jit(solution)/shard_map/ppermute | solution.py:57
  65.3 5.1 %collective-permute-start.2 = (bf16[8,128,256]{2,1,0:T(8,128)(2,1)S(1)}, bf16[8,128,256]{2,1,0:T(8,128)(2,1)}, u32[]{:S(2)}, u32[]{:S(2)}) collective-permute-start(bf16[8,128,256]{2,1,0:T(8,128)(2,1)S(1)} %collective-permute-done.1.w2), channel_id=1, source_target_pairs={{0,56},{8,0},{16,8},{24,16},{32,24},{40,32},{48,40},{56,48},{64,12... | collective-permute-start | bytes 1572872 | tf_op jit(solution)/shard_map/ppermute | solution.py:57
  70.5 0.7 compare_select_fusion
  71.8 0.9 copy.21
  72.7 0.8 copy.15.alevels_ref
  74.1 0.9 multiply_convert_fusion
  74.9 0.9 pad_maximum_fusion.rows_ref
  76.5 0.7 collective-permute-done.2.w3
  77.1 10.2 %shard_map.130 = (bf16[128,256]{1,0:T(8,128)(2,1)}, f32[128,256]{1,0:T(8,128)}, f32[128,256]{1,0:T(8,128)S(1)}, bf16[8,8,256,128]{3,2,1,0:T(8,128)(2,1)}) custom-call(bf16[512,8192]{1,0:T(8,128)(2,1)} %all-gather.2.cloned.1.call-done.normed_ref, bf16[8,128,256]{2,1,0:T(8,128)(2,1)S(1)} %all_to_all.10.w0, bf16[8,128,256]{2,1,0:T(8,128)(2,1)S(1)} %collective-permute-done.w1, ...), custom_call_target="tpu_custom_call" | custom-call | flops 4294967296 | bytes 16777216 | tf_op jit(solution)/shard_map/pallas_call | solution.py:222
  87.3 40.6 %reduce-scatter.2.cloned.1.call-done = bf16[2048,128]{1,0:T(8,128)(2,1)} async-done(((bf16[16384,128]{1,0:T(8,128)(2,1)}), bf16[2048,128]{1,0:T(8,128)(2,1)}) %reduce-scatter.2.cloned.1.call-update) | async-done | bytes 524304 | tf_op jit(solution)/shard_map/reduce_scatter | solution.py:282
  127.9 20.7 %all_to_all.11 = bf16[8,256,128]{2,1,0:T(8,128)(2,1)S(1)} all-to-all(bf16[8,256,128]{2,1,0:T(8,128)(2,1)} %bitcast.24), channel_id=1, replica_groups={{0,64,128,192,256,320,384,448},{8,72,136,200,264,328,392,456},{16,80,14..., dimensions={0} | all-to-all | bytes 1048576 | tf_op jit(solution)/shard_map/all_to_all | solution.py:48
  148.7 3.0 %collective-permute-start.7 = (bf16[256,128]{1,0:T(8,128)(2,1)S(1)}, bf16[256,128]{1,0:T(8,128)(2,1)S(1)}, u32[]{:S(2)}, u32[]{:S(2)}) collective-permute-start(bf16[256,128]{1,0:T(8,128)(2,1)S(1)} %reduce_sum.12), channel_id=1, source_target_pairs={{0,8},{8,0},{1,9},{9,1},{2,10},{10,2},{3,11},{11,3},{4,12},{12,4},... | collective-permute-start | bytes 196616 | tf_op jit(solution)/shard_map/ppermute | solution.py:291
  151.7 0.7 reshape.50
  152.4 2.4 %collective-permute-done.7 = bf16[256,128]{1,0:T(8,128)(2,1)S(1)} collective-permute-done((bf16[256,128]{1,0:T(8,128)(2,1)S(1)}, bf16[256,128]{1,0:T(8,128)(2,1)S(1)}, u32[]{:S(2)}, u32[]{:S(2)}) %collective-permute-start.7) | collective-permute-done | bytes 65568 | tf_op jit(solution)/shard_map/ppermute | solution.py:291
  154.9 0.8 copy.16
  (19 shorter events, 1.9 us)
Async XLA Ops:
  7.2 2.7 %copy-start = (bf16[256,2,128]{2,1,0:T(2,128)(2,1)S(1)}, bf16[256,2,128]{2,1,0:T(2,128)(2,1)}, u32[]{:S(2)}) copy-start(bf16[256,2,128]{2,1,0:T(2,128)(2,1)} %param.12) | copy-start | bytes 393220
  7.2 70.0 %all-gather.2.cloned.1.call-start = ((), (), s32[]{:S(2)}) async-start(), calls=%async_computation.3 | async-start | bytes 9437184 | tf_op jit(solution)/shard_map/all_gather | solution.py:263
  9.8 118.1 %reduce-scatter.2.cloned.1.call-start = ((), (), s32[]{:S(2)}) async-start(), calls=%async_computation.4 | async-start | bytes 4718592 | tf_op jit(solution)/shard_map/reduce_scatter | solution.py:282
  33.4 16.1 %collective-permute-start.3 = (bf16[8,128,256]{2,1,0:T(8,128)(2,1)S(1)}, bf16[8,128,256]{2,1,0:T(8,128)(2,1)S(1)}, u32[]{:S(2)}, u32[]{:S(2)}) collective-permute-start(bf16[8,128,256]{2,1,0:T(8,128)(2,1)S(1)} %all_to_all.10.w0), channel_id=1, source_target_pairs={{0,16},{8,24},{16,32},{24,40},{32,48},{40,56},{48,0},{56,8},{64,80... | collective-permute-start | bytes 1572872 | tf_op jit(solution)/shard_map/ppermute | solution.py:57
  37.9 18.6 %collective-permute-start.1 = (bf16[8,128,256]{2,1,0:T(8,128)(2,1)S(1)}, bf16[8,128,256]{2,1,0:T(8,128)(2,1)S(1)}, u32[]{:S(2)}, u32[]{:S(2)}) collective-permute-start(bf16[8,128,256]{2,1,0:T(8,128)(2,1)S(1)} %all_to_all.10.w0), channel_id=1, source_target_pairs={{0,48},{8,56},{16,0},{24,8},{32,16},{40,24},{48,32},{56,40},{64,11... | collective-permute-start | bytes 1572872 | tf_op jit(solution)/shard_map/ppermute | solution.py:57
  42.2 33.6 %collective-permute-start.6 = (bf16[8,128,256]{2,1,0:T(8,128)(2,1)S(1)}, bf16[8,128,256]{2,1,0:T(8,128)(2,1)S(1)}, u32[]{:S(2)}, u32[]{:S(2)}) collective-permute-start(bf16[8,128,256]{2,1,0:T(8,128)(2,1)S(1)} %all_to_all.10.w0), channel_id=1, source_target_pairs={{0,8},{8,16},{16,24},{24,32},{32,40},{40,48},{48,56},{56,0},{64,72... | collective-permute-start | bytes 1572872 | tf_op jit(solution)/shard_map/ppermute | solution.py:57
  45.5 30.3 %collective-permute-start = (bf16[8,128,256]{2,1,0:T(8,128)(2,1)S(1)}, bf16[8,128,256]{2,1,0:T(8,128)(2,1)S(1)}, u32[]{:S(2)}, u32[]{:S(2)}) collective-permute-start(bf16[8,128,256]{2,1,0:T(8,128)(2,1)S(1)} %all_to_all.10.w0), channel_id=1, source_target_pairs={{0,56},{8,0},{16,8},{24,16},{32,24},{40,32},{48,40},{56,48},{64,12... | collective-permute-start | bytes 1572872 | tf_op jit(solution)/shard_map/ppermute | solution.py:57
  57.3 19.1 %collective-permute-start.4 = (bf16[8,128,256]{2,1,0:T(8,128)(2,1)}, bf16[8,128,256]{2,1,0:T(8,128)(2,1)}, u32[]{:S(2)}, u32[]{:S(2)}) collective-permute-start(bf16[8,128,256]{2,1,0:T(8,128)(2,1)} %broadcast_select_fusion), channel_id=1, source_target_pairs={{0,16},{8,56},{16,32},{24,8},{32,48},{40,24},{48,0},{56,40},{64,80... | collective-permute-start | bytes 1572872 | tf_op jit(solution)/shard_map/ppermute | solution.py:73
  63.4 13.1 %collective-permute-start.5 = (bf16[8,128,256]{2,1,0:T(8,128)(2,1)S(1)}, bf16[8,128,256]{2,1,0:T(8,128)(2,1)}, u32[]{:S(2)}, u32[]{:S(2)}) collective-permute-start(bf16[8,128,256]{2,1,0:T(8,128)(2,1)S(1)} %collective-permute-done.3.w6), channel_id=1, source_target_pairs={{0,8},{8,16},{16,24},{24,32},{32,40},{40,48},{48,56},{56,0},{64,72... | collective-permute-start | bytes 1572872 | tf_op jit(solution)/shard_map/ppermute | solution.py:57
  65.3 11.8 %collective-permute-start.2 = (bf16[8,128,256]{2,1,0:T(8,128)(2,1)S(1)}, bf16[8,128,256]{2,1,0:T(8,128)(2,1)}, u32[]{:S(2)}, u32[]{:S(2)}) collective-permute-start(bf16[8,128,256]{2,1,0:T(8,128)(2,1)S(1)} %collective-permute-done.1.w2), channel_id=1, source_target_pairs={{0,56},{8,0},{16,8},{24,16},{32,24},{40,32},{48,40},{56,48},{64,12... | collective-permute-start | bytes 1572872 | tf_op jit(solution)/shard_map/ppermute | solution.py:57
  148.7 6.2 %collective-permute-start.7 = (bf16[256,128]{1,0:T(8,128)(2,1)S(1)}, bf16[256,128]{1,0:T(8,128)(2,1)S(1)}, u32[]{:S(2)}, u32[]{:S(2)}) collective-permute-start(bf16[256,128]{1,0:T(8,128)(2,1)S(1)} %reduce_sum.12), channel_id=1, source_target_pairs={{0,8},{8,0},{1,9},{9,1},{2,10},{10,2},{3,11},{11,3},{4,12},{12,4},... | collective-permute-start | bytes 196616 | tf_op jit(solution)/shard_map/ppermute | solution.py:291
Sparse Core Ops, SparseCore 0:
  10.2 58.8 all-gather.1
  87.4 40.4 reduce-scatter.1

commit v5 on v4

--- a/solution.py
+++ b/solution.py
@@ -57,11 +57,13 @@
     return lax.ppermute(array, EVERY, pairs)
 
 
-def around(array, groups, place):
+def around(array, groups, place, raw, prepare):
     behind2 = shifted(array, groups, 2)
     ahead2 = shifted(array, groups, -2)
     behind1 = shifted(array, groups, 1)
     ahead1 = shifted(array, groups, -1)
+    behind2, raw = lax.optimization_barrier((behind2, raw))
+    ahead2, others = lax.optimization_barrier((ahead2, prepare(*raw)))
     behind3 = shifted(behind2, groups, 1)
     ahead3 = shifted(ahead2, groups, -1)
     even = place % 2 == 0
@@ -71,7 +73,8 @@
         for k in range(RING)
     ]
     opposite = lax.ppermute(jnp.where(even, behind2, ahead2), EVERY, onward)
-    return (array, ahead1, ahead2, ahead3, opposite, behind3, behind2, behind1)
+    weights = (array, ahead1, ahead2, ahead3, opposite, behind3, behind2, behind1)
+    return weights, others
 
 
 def norm_kernel(hidden_ref, gain_ref, out_ref):
@@ -245,6 +248,19 @@
     )(normed, *weights, rows, pair, levels, alevels)
 
 
+def prepare(query, pair, cotangent, prefix_blocks, action_blocks, prefix_lengths, timesteps):
+    flow_weight = 0.5 + (timesteps[0].astype(jnp.float32) + 0.5) / STEPS
+    grad_out = (flow_weight * cotangent[0].astype(jnp.float32)).astype(jnp.bfloat16)
+    positions = jnp.arange(PREFIX, dtype=jnp.int32)
+    levels = jnp.where(positions[None, :] < prefix_lengths[0], prefix_blocks, UNSEEN)
+    return (
+        jnp.stack([query[0], grad_out]),
+        pair[0].reshape(ACT, COLUMNS),
+        jnp.concatenate([levels, action_blocks], axis=1),
+        action_blocks.reshape(ACT, 1),
+    )
+
+
 def shards(
     prefix_hidden,
     norm_gain,
@@ -265,20 +281,17 @@
     line = exchange(jnp.broadcast_to(local, (RING, *local.shape)), FIRST)
     core = lax.axis_index("mp") % 2
     place = jnp.where(core == 0, lax.axis_index("dp_1") * 2 + side, lax.axis_index("dp_0"))
-    weights = around(line, SECOND, place)
-    flow_weight = 0.5 + (timesteps[0].astype(jnp.float32) + 0.5) / STEPS
-    grad_out = (flow_weight * out_cotangent[0].astype(jnp.float32)).astype(jnp.bfloat16)
-    positions = jnp.arange(PREFIX, dtype=jnp.int32)
-    levels = jnp.where(positions[None, :] < prefix_lengths[0], prefix_blocks, UNSEEN)
-    levels = jnp.concatenate([levels, action_blocks], axis=1)
-    out, d_query, d_action, term = attend(
-        normed,
-        weights,
-        jnp.stack([action_query[0], grad_out]),
-        action_kv[0].reshape(ACT, COLUMNS),
-        levels,
-        action_blocks.reshape(ACT, 1),
-    )
+    raw = (
+        action_query,
+        action_kv,
+        out_cotangent,
+        prefix_blocks,
+        action_blocks,
+        prefix_lengths,
+        timesteps,
+    )
+    weights, others = around(line, SECOND, place, raw, prepare)
+    out, d_query, d_action, term = attend(normed, weights, *others)
     ring_sum = lax.psum_scatter(
         term.reshape(RING * RING * COLUMNS, PART),
         EVERY,

time: 163 us -> 167 us (1.025)
  waiting for transfers between devices: 51.6 us -> 55.9 us
    ppermute x1, waiting for transfers between devices: 0.01 us -> 5.47 us  [around(): opposite = lax.ppermute(jnp.where(even, behind2, ahead2), EVERY, onward)]
    ppermute x1, starting transfers between devices: 6.02 us -> 3.49 us  [around(): opposite = lax.ppermute(jnp.where(even, behind2, ahead2), EVERY, onward)]
    ppermute x6, starting transfers between devices: 22.2 us -> 24 us  [shifted(): return lax.ppermute(array, EVERY, pairs)]
  transfers between devices with their start and end apart: 10 -> 10, of which waited for: 6 -> 5; matrix products, arithmetic and copies ran while one was open for 4% -> 4% of each run, Pallas kernels for 0% -> 0%
where the time goes in v5:
time: 167 us; the launch traced here: 166 us
  waiting for transfers between devices  55.9 us (33%)
  blocking collectives  44.1 us (26%)
  starting transfers between devices  30.7 us (18%)
  between operations  15.5 us (9%)
  Pallas kernels  12.7 us (8%)
  other arithmetic  4.03 us (2%)
  local copies, waits for them, and re-layouts  3.28 us (2%)
    all_to_all x2, blocking collectives, exchange(): lax.all_to_all(parts, EVERY, split_axis=0, concat_axis=0, tiled=True, axi...  44.1 us
    reduce_scatter x1, waiting for transfers between devices, shards(): lax.psum_scatter(term.reshape(RING * RING * COLUMNS, PART), EVERY, scatte...  41 us
    ppermute x6, starting transfers between devices, shifted(): return lax.ppermute(array, EVERY, pairs)  24 us
    pallas_call x1, Pallas kernels, attend(): pl.pallas_call(attend_kernel, out_shape=(jax.ShapeDtypeStruct((ACT, COLUM...  10.1 us
    ppermute x6, waiting for transfers between devices, shifted(): return lax.ppermute(array, EVERY, pairs)  7.06 us
    ppermute x1, waiting for transfers between devices, around(): opposite = lax.ppermute(jnp.where(even, behind2, ahead2), EVERY, onward)  5.47 us
    ppermute x1, starting transfers between devices, around(): opposite = lax.ppermute(jnp.where(even, behind2, ahead2), EVERY, onward)  3.49 us
  transfers between devices with their start and end apart: 10, of which 5 were waited for; matrix products, arithmetic and copies ran while one was open for 4% of the time, Pallas kernels for 0%

profile of v5, /device:TPU:2, one launch (start us, length us, event | category | flops | bytes accessed | tf_op | source)
XLA Modules:
  0.0 166.2 jit_solution(17092318483197544516)
XLA Ops:
  7.2 2.6 %shard_map.129 = bf16[64,8192]{1,0:T(8,128)(2,1)} custom-call(bf16[1,64,8192]{2,1,0:T(8,128)(2,1)} %hidden_ref.1, f32[1,8192]{1,0:T(1,128)} %bitcast.28), custom_call_target="tpu_custom_call" | custom-call | flops 2097152 | bytes 2097152 | tf_op jit(solution)/shard_map/pallas_call | solution.py:88
  10.0 23.4 %all_to_all.10.w0 = bf16[8,128,256]{2,1,0:T(8,128)(2,1)S(1)} all-to-all(bf16[8,128,256]{2,1,0:T(8,128)(2,1)S(1)} %broadcast_in_dim.14), channel_id=1, replica_groups={{0,64,128,192,256,320,384,448},{8,72,136,200,264,328,392,456},{16,80,14..., dimensions={0} | all-to-all | bytes 1048576 | tf_op jit(solution)/shard_map/all_to_all | solution.py:48
  33.4 4.5 %collective-permute-start.2 = (bf16[8,128,256]{2,1,0:T(8,128)(2,1)S(1)}, bf16[8,128,256]{2,1,0:T(8,128)(2,1)S(1)}, u32[]{:S(2)}, u32[]{:S(2)}) collective-permute-start(bf16[8,128,256]{2,1,0:T(8,128)(2,1)S(1)} %all_to_all.10.w0), channel_id=1, source_target_pairs={{0,16},{8,24},{16,32},{24,40},{32,48},{40,56},{48,0},{56,8},{64,80... | collective-permute-start | bytes 1572872 | tf_op jit(solution)/shard_map/ppermute | solution.py:57
  39.2 3.5 %collective-permute-start.6 = (bf16[8,128,256]{2,1,0:T(8,128)(2,1)S(1)}, bf16[8,128,256]{2,1,0:T(8,128)(2,1)S(1)}, u32[]{:S(2)}, u32[]{:S(2)}) collective-permute-start(bf16[8,128,256]{2,1,0:T(8,128)(2,1)S(1)} %all_to_all.10.w0), channel_id=1, source_target_pairs={{0,8},{8,16},{16,24},{24,32},{32,40},{40,48},{48,56},{56,0},{64,72... | collective-permute-start | bytes 1572872 | tf_op jit(solution)/shard_map/ppermute | solution.py:57
  42.7 3.5 %collective-permute-start.1 = (bf16[8,128,256]{2,1,0:T(8,128)(2,1)S(1)}, bf16[8,128,256]{2,1,0:T(8,128)(2,1)S(1)}, u32[]{:S(2)}, u32[]{:S(2)}) collective-permute-start(bf16[8,128,256]{2,1,0:T(8,128)(2,1)S(1)} %all_to_all.10.w0), channel_id=1, source_target_pairs={{0,48},{8,56},{16,0},{24,8},{32,16},{40,24},{48,32},{56,40},{64,11... | collective-permute-start | bytes 1572872 | tf_op jit(solution)/shard_map/ppermute | solution.py:57
  46.2 2.6 %collective-permute-start = (bf16[8,128,256]{2,1,0:T(8,128)(2,1)S(1)}, bf16[8,128,256]{2,1,0:T(8,128)(2,1)S(1)}, u32[]{:S(2)}, u32[]{:S(2)}) collective-permute-start(bf16[8,128,256]{2,1,0:T(8,128)(2,1)S(1)} %all_to_all.10.w0), channel_id=1, source_target_pairs={{0,56},{8,0},{16,8},{24,16},{32,24},{40,32},{48,40},{56,48},{64,12... | collective-permute-start | bytes 1572872 | tf_op jit(solution)/shard_map/ppermute | solution.py:57
  48.8 0.7 collective-permute-done.2.w6
  49.5 0.9 copy.21
  50.4 6.3 %collective-permute-start.5 = (bf16[8,128,256]{2,1,0:T(8,128)(2,1)S(1)}, bf16[8,128,256]{2,1,0:T(8,128)(2,1)}, u32[]{:S(2)}, u32[]{:S(2)}) collective-permute-start(bf16[8,128,256]{2,1,0:T(8,128)(2,1)S(1)} %collective-permute-done.2.w6), channel_id=1, source_target_pairs={{0,8},{8,16},{16,24},{24,32},{32,40},{40,48},{48,56},{56,0},{64,72... | collective-permute-start | bytes 1572872 | tf_op jit(solution)/shard_map/ppermute | solution.py:57
  58.0 0.9 multiply_convert_fusion
  58.9 0.9 pad_maximum_fusion.rows_ref
  59.7 0.9 broadcast_select_fusion
  60.6 3.5 %collective-permute-start.4 = (bf16[8,128,256]{2,1,0:T(8,128)(2,1)}, bf16[8,128,256]{2,1,0:T(8,128)(2,1)}, u32[]{:S(2)}, u32[]{:S(2)}) collective-permute-start(bf16[8,128,256]{2,1,0:T(8,128)(2,1)} %broadcast_select_fusion), channel_id=1, source_target_pairs={{0,16},{8,56},{16,32},{24,8},{32,48},{40,24},{48,0},{56,40},{64,80... | collective-permute-start | bytes 1572872 | tf_op jit(solution)/shard_map/ppermute | solution.py:75
  64.1 3.7 %collective-permute-start.3 = (bf16[8,128,256]{2,1,0:T(8,128)(2,1)S(1)}, bf16[8,128,256]{2,1,0:T(8,128)(2,1)}, u32[]{:S(2)}, u32[]{:S(2)}) collective-permute-start(bf16[8,128,256]{2,1,0:T(8,128)(2,1)S(1)} %collective-permute-done.1.w2), channel_id=1, source_target_pairs={{0,56},{8,0},{16,8},{24,16},{32,24},{40,32},{48,40},{56,48},{64,12... | collective-permute-start | bytes 1572872 | tf_op jit(solution)/shard_map/ppermute | solution.py:57
  67.8 0.8 copy.15.alevels_ref
  68.6 5.5 %collective-permute-done.4.w4 = bf16[8,128,256]{2,1,0:T(8,128)(2,1)} collective-permute-done((bf16[8,128,256]{2,1,0:T(8,128)(2,1)}, bf16[8,128,256]{2,1,0:T(8,128)(2,1)}, u32[]{:S(2)}, u32[]{:S(2)}) %collective-permute-start.4) | collective-permute-done | bytes 524320 | tf_op jit(solution)/shard_map/ppermute | solution.py:75
  74.1 6.3 %collective-permute-done.3.w3 = bf16[8,128,256]{2,1,0:T(8,128)(2,1)} collective-permute-done((bf16[8,128,256]{2,1,0:T(8,128)(2,1)S(1)}, bf16[8,128,256]{2,1,0:T(8,128)(2,1)}, u32[]{:S(2)}, u32[]{:S(2)}) %collective-permute-start.3) | collective-permute-done | bytes 524320 | tf_op jit(solution)/shard_map/ppermute | solution.py:57
  80.4 10.1 %shard_map.130 = (bf16[128,256]{1,0:T(8,128)(2,1)}, f32[128,256]{1,0:T(8,128)}, f32[128,256]{1,0:T(8,128)S(1)}, bf16[8,8,256,128]{3,2,1,0:T(8,128)(2,1)}) custom-call(bf16[512,8192]{1,0:T(8,128)(2,1)} %all-gather.2.cloned.1.call-done.normed_ref, bf16[8,128,256]{2,1,0:T(8,128)(2,1)S(1)} %all_to_all.10.w0, bf16[8,128,256]{2,1,0:T(8,128)(2,1)S(1)} %collective-permute-done.w1, ...), custom_call_target="tpu_custom_call" | custom-call | flops 4294967296 | bytes 16777216 | tf_op jit(solution)/shard_map/pallas_call | solution.py:225
  90.6 41.0 %reduce-scatter.2.cloned.1.call-done = bf16[2048,128]{1,0:T(8,128)(2,1)} async-done(((bf16[16384,128]{1,0:T(8,128)(2,1)}), bf16[2048,128]{1,0:T(8,128)(2,1)}) %reduce-scatter.2.cloned.1.call-update) | async-done | bytes 524304 | tf_op jit(solution)/shard_map/reduce_scatter | solution.py:295
  131.6 20.6 %all_to_all.11 = bf16[8,256,128]{2,1,0:T(8,128)(2,1)S(1)} all-to-all(bf16[8,256,128]{2,1,0:T(8,128)(2,1)} %bitcast.24), channel_id=1, replica_groups={{0,64,128,192,256,320,384,448},{8,72,136,200,264,328,392,456},{16,80,14..., dimensions={0} | all-to-all | bytes 1048576 | tf_op jit(solution)/shard_map/all_to_all | solution.py:48
  152.3 3.1 %collective-permute-start.7 = (bf16[256,128]{1,0:T(8,128)(2,1)S(1)}, bf16[256,128]{1,0:T(8,128)(2,1)S(1)}, u32[]{:S(2)}, u32[]{:S(2)}) collective-permute-start(bf16[256,128]{1,0:T(8,128)(2,1)S(1)} %reduce_sum.12), channel_id=1, source_target_pairs={{0,8},{8,0},{1,9},{9,1},{2,10},{10,2},{3,11},{11,3},{4,12},{12,4},... | collective-permute-start | bytes 196616 | tf_op jit(solution)/shard_map/ppermute | solution.py:304
  155.4 0.7 reshape.50
  156.1 2.3 %collective-permute-done.7 = bf16[256,128]{1,0:T(8,128)(2,1)S(1)} collective-permute-done((bf16[256,128]{1,0:T(8,128)(2,1)S(1)}, bf16[256,128]{1,0:T(8,128)(2,1)S(1)}, u32[]{:S(2)}, u32[]{:S(2)}) %collective-permute-start.7) | collective-permute-done | bytes 65568 | tf_op jit(solution)/shard_map/ppermute | solution.py:304
  158.5 0.8 copy.16
  (19 shorter events, 1.7 us)
Async XLA Ops:
  7.2 2.7 %copy-start = (bf16[256,2,128]{2,1,0:T(2,128)(2,1)S(1)}, bf16[256,2,128]{2,1,0:T(2,128)(2,1)}, u32[]{:S(2)}) copy-start(bf16[256,2,128]{2,1,0:T(2,128)(2,1)} %param.12) | copy-start | bytes 393220
  7.2 73.3 %all-gather.2.cloned.1.call-start = ((), (), s32[]{:S(2)}) async-start(), calls=%async_computation.3 | async-start | bytes 9437184 | tf_op jit(solution)/shard_map/all_gather | solution.py:279
  9.8 121.8 %reduce-scatter.2.cloned.1.call-start = ((), (), s32[]{:S(2)}) async-start(), calls=%async_computation.4 | async-start | bytes 4718592 | tf_op jit(solution)/shard_map/reduce_scatter | solution.py:295
  33.4 16.1 %collective-permute-start.2 = (bf16[8,128,256]{2,1,0:T(8,128)(2,1)S(1)}, bf16[8,128,256]{2,1,0:T(8,128)(2,1)S(1)}, u32[]{:S(2)}, u32[]{:S(2)}) collective-permute-start(bf16[8,128,256]{2,1,0:T(8,128)(2,1)S(1)} %all_to_all.10.w0), channel_id=1, source_target_pairs={{0,16},{8,24},{16,32},{24,40},{32,48},{40,56},{48,0},{56,8},{64,80... | collective-permute-start | bytes 1572872 | tf_op jit(solution)/shard_map/ppermute | solution.py:57
  39.2 29.4 %collective-permute-start.6 = (bf16[8,128,256]{2,1,0:T(8,128)(2,1)S(1)}, bf16[8,128,256]{2,1,0:T(8,128)(2,1)S(1)}, u32[]{:S(2)}, u32[]{:S(2)}) collective-permute-start(bf16[8,128,256]{2,1,0:T(8,128)(2,1)S(1)} %all_to_all.10.w0), channel_id=1, source_target_pairs={{0,8},{8,16},{16,24},{24,32},{32,40},{40,48},{48,56},{56,0},{64,72... | collective-permute-start | bytes 1572872 | tf_op jit(solution)/shard_map/ppermute | solution.py:57
  42.7 17.0 %collective-permute-start.1 = (bf16[8,128,256]{2,1,0:T(8,128)(2,1)S(1)}, bf16[8,128,256]{2,1,0:T(8,128)(2,1)S(1)}, u32[]{:S(2)}, u32[]{:S(2)}) collective-permute-start(bf16[8,128,256]{2,1,0:T(8,128)(2,1)S(1)} %all_to_all.10.w0), channel_id=1, source_target_pairs={{0,48},{8,56},{16,0},{24,8},{32,16},{40,24},{48,32},{56,40},{64,11... | collective-permute-start | bytes 1572872 | tf_op jit(solution)/shard_map/ppermute | solution.py:57
  46.2 22.4 %collective-permute-start = (bf16[8,128,256]{2,1,0:T(8,128)(2,1)S(1)}, bf16[8,128,256]{2,1,0:T(8,128)(2,1)S(1)}, u32[]{:S(2)}, u32[]{:S(2)}) collective-permute-start(bf16[8,128,256]{2,1,0:T(8,128)(2,1)S(1)} %all_to_all.10.w0), channel_id=1, source_target_pairs={{0,56},{8,0},{16,8},{24,16},{32,24},{40,32},{48,40},{56,48},{64,12... | collective-permute-start | bytes 1572872 | tf_op jit(solution)/shard_map/ppermute | solution.py:57
  50.4 18.2 %collective-permute-start.5 = (bf16[8,128,256]{2,1,0:T(8,128)(2,1)S(1)}, bf16[8,128,256]{2,1,0:T(8,128)(2,1)}, u32[]{:S(2)}, u32[]{:S(2)}) collective-permute-start(bf16[8,128,256]{2,1,0:T(8,128)(2,1)S(1)} %collective-permute-done.2.w6), channel_id=1, source_target_pairs={{0,8},{8,16},{16,24},{24,32},{32,40},{40,48},{48,56},{56,0},{64,72... | collective-permute-start | bytes 1572872 | tf_op jit(solution)/shard_map/ppermute | solution.py:57
  60.6 13.5 %collective-permute-start.4 = (bf16[8,128,256]{2,1,0:T(8,128)(2,1)}, bf16[8,128,256]{2,1,0:T(8,128)(2,1)}, u32[]{:S(2)}, u32[]{:S(2)}) collective-permute-start(bf16[8,128,256]{2,1,0:T(8,128)(2,1)} %broadcast_select_fusion), channel_id=1, source_target_pairs={{0,16},{8,56},{16,32},{24,8},{32,48},{40,24},{48,0},{56,40},{64,80... | collective-permute-start | bytes 1572872 | tf_op jit(solution)/shard_map/ppermute | solution.py:75
  64.1 16.3 %collective-permute-start.3 = (bf16[8,128,256]{2,1,0:T(8,128)(2,1)S(1)}, bf16[8,128,256]{2,1,0:T(8,128)(2,1)}, u32[]{:S(2)}, u32[]{:S(2)}) collective-permute-start(bf16[8,128,256]{2,1,0:T(8,128)(2,1)S(1)} %collective-permute-done.1.w2), channel_id=1, source_target_pairs={{0,56},{8,0},{16,8},{24,16},{32,24},{40,32},{48,40},{56,48},{64,12... | collective-permute-start | bytes 1572872 | tf_op jit(solution)/shard_map/ppermute | solution.py:57
  152.3 6.2 %collective-permute-start.7 = (bf16[256,128]{1,0:T(8,128)(2,1)S(1)}, bf16[256,128]{1,0:T(8,128)(2,1)S(1)}, u32[]{:S(2)}, u32[]{:S(2)}) collective-permute-start(bf16[256,128]{1,0:T(8,128)(2,1)S(1)} %reduce_sum.12), channel_id=1, source_target_pairs={{0,8},{8,0},{1,9},{9,1},{2,10},{10,2},{3,11},{11,3},{4,12},{12,4},... | collective-permute-start | bytes 196616 | tf_op jit(solution)/shard_map/ppermute | solution.py:304
Sparse Core Ops, SparseCore 0:
  10.2 58.8 all-gather.1
  90.7 40.8 reduce-scatter.1
